TPU v7x, 32 devices: a whole 2x2x4 slice. The times are simulated.
32 devices in a mesh: dp: 16 (over z, y, x), tensor: 2 (over core).
Axes of the slice: x: 2, y: 2, z: 4, core: 2. Of those that a mesh axis runs over, the one named last changes fastest.
Arguments:
- hidden: float32 [32768, 768], P('dp'), may hold values from -6 to 6
- cotangent: float32 [32768, 768], P('dp'), may hold values from -6 to 6
- norm_weight: float32 [768], replicated, may hold values from 0.5 to 1.5
- gate_in: bfloat16 [768, 1536], P(None, 'tensor'), may hold values from -0.21875 to 0.21875
- value_in: bfloat16 [768, 1536], P(None, 'tensor'), may hold values from -0.21875 to 0.21875
- state_in: bfloat16 [768, 256], replicated, may hold values from -0.21875 to 0.21875
- step_in: bfloat16 [768, 24], P(None, 'tensor'), may hold values from -0.21875 to 0.21875
- value_kernel: float32 [4, 1536], P(None, 'tensor'), may hold values from -3 to 3
- value_offset: float32 [1536], P('tensor'), may hold values from -0.5 to 0.5
- state_kernel: float32 [4, 256], replicated, may hold values from -3 to 3
- state_offset: float32 [256], replicated, may hold values from -0.5 to 0.5
- step_bias: float32 [24], P('tensor'), may hold values from -5 to -2
- log_decay: float32 [24], P('tensor'), may hold values from -3 to 0
- skip_weight: float32 [24], P('tensor'), may hold values from 0.5 to 1.5
- gated_norm: float32 [1536], P('tensor'), may hold values from 0.5 to 1.5
- out_weight: bfloat16 [1536, 768], P('tensor'), may hold values from -0.15625 to 0.15625
Outputs:
- block_out: float32 [32768, 768], P('dp')
- grad_hidden: float32 [32768, 768], P('dp')
- grad_norm_weight: float32 [768], replicated
- grad_gate_in: float32 [768, 1536], P(None, 'tensor')
- grad_value_in: float32 [768, 1536], P(None, 'tensor')
- grad_state_in: float32 [768, 256], replicated
- grad_step_in: float32 [768, 24], P(None, 'tensor')
- grad_value_kernel: float32 [4, 1536], P(None, 'tensor')
- grad_value_offset: float32 [1536], P('tensor')
- grad_state_kernel: float32 [4, 256], replicated
- grad_state_offset: float32 [256], replicated
- grad_step_bias: float32 [24], P('tensor')
- grad_log_decay: float32 [24], P('tensor')
- grad_skip_weight: float32 [24], P('tensor')
- grad_gated_norm: float32 [1536], P('tensor')
- grad_out_weight: float32 [1536, 768], P('tensor')
All inputs are finite; a program needn't handle non-finite values.
Results may differ from a plain program's by a relative error of at most 0.0081.
Values sent between devices are 32-bit elements; how exact they have to be, the bound alone decides.
No kernel may reach another device: no remote copies, remote signals or barrier semaphores. Data moves between devices by JAX's collectives and lax.ppermute only.
A program may use at most 192 MiB of HBM per device.

v0:
```python
import jax
import jax.numpy as jnp
from jax import lax
from jax.sharding import PartitionSpec as P

HEADS = 24
HEAD_DIM = 64
STATE = 128
BLOCK = 256
LENGTH = 512


EPSILON = 1e-05
HIGHEST = lax.Precision.HIGHEST


def conv_silu(series, kernel, kernel_bias):
    tap_count = kernel.shape[0]
    positions = series.shape[1]
    padded = jnp.pad(series, ((0, 0), (tap_count - 1, 0), (0, 0)))
    summed = kernel_bias + kernel[0] * padded[:, 0:positions]
    for offset in range(1, tap_count):
        summed = summed + kernel[offset] * padded[:, offset : offset + positions]
    return jax.nn.silu(summed)


def state_scan(values, write_rows, read_rows, step_sizes, decay_rates):
    block_size = values.shape[1]
    log_steps = step_sizes * decay_rates
    running = jnp.cumsum(log_steps, axis=1)
    causal = jnp.arange(block_size)[:, None] >= jnp.arange(block_size)[None, :]
    log_gaps = running[:, :, None, :] - running[:, None, :, :]
    pair_decay = jnp.exp(jnp.where(causal[None, :, :, None], log_gaps, -1e30))
    intersections = jnp.einsum("bin,bjn->bij", read_rows, write_rows, precision=HIGHEST)
    mixing = intersections[:, :, :, None] * pair_decay * step_sizes[:, None, :, :]
    within = jnp.einsum("bijh,bjhp->bihp", mixing, values, precision=HIGHEST)
    tail_decay = jnp.exp(running[:, -1:, :] - running) * step_sizes
    block_states = jnp.einsum(
        "bjh,bjhp,bjn->bhpn", tail_decay, values, write_rows, precision=HIGHEST
    )
    block_decay = jnp.exp(running[:, -1, :])

    def carry_state(carried, element):
        block_state, block_factor = element
        return (block_factor[:, None, None] * carried + block_state, carried)

    initial = jnp.zeros(block_states.shape[1:], jnp.float32)
    final_state, entering = lax.scan(carry_state, initial, (block_states, block_decay))
    across = (
        jnp.einsum("bin,bhpn->bihp", read_rows, entering, precision=HIGHEST)
        * jnp.exp(running)[:, :, :, None]
    )
    return within + across


def mix_heads(
    value_raw,
    step_raw,
    gate_raw,
    state_inputs,
    value_kernel,
    value_offset,
    step_bias,
    log_decay,
    skip_weight,
):
    token_count = value_raw.shape[0]
    channels = value_raw.shape[1]
    head_count = step_raw.shape[1]
    sequences = token_count // LENGTH
    blocks = LENGTH // BLOCK
    conv_values = conv_silu(
        value_raw.reshape(sequences, LENGTH, channels), value_kernel, value_offset
    )
    step_sizes = jax.nn.softplus(step_raw + step_bias).reshape(sequences, blocks, BLOCK, head_count)
    per_head = conv_values.reshape(sequences, blocks, BLOCK, head_count, HEAD_DIM)
    write_rows = state_inputs[:, :, :STATE].reshape(sequences, blocks, BLOCK, STATE)
    read_rows = state_inputs[:, :, STATE:].reshape(sequences, blocks, BLOCK, STATE)
    decay_rates = -jnp.exp(log_decay)
    scanned = jax.vmap(state_scan, in_axes=(0, 0, 0, 0, None))(
        per_head, write_rows, read_rows, step_sizes, decay_rates
    )
    direct = per_head * skip_weight[:, None]
    mixed_rows = scanned.reshape(token_count, channels) + direct.reshape(token_count, channels)
    return mixed_rows * jax.nn.silu(gate_raw)


def state_branch(state_raw, state_kernel, state_offset):
    return conv_silu(state_raw.reshape(-1, LENGTH, state_raw.shape[1]), state_kernel, state_offset)


def transposed_left(left_side, right_side):
    return lax.dot_general(
        left_side, right_side, (((0,), (0,)), ((), ())), preferred_element_type=jnp.float32
    )


def transposed_right(left_side, right_side):
    return lax.dot_general(
        left_side, right_side, (((1,), (1,)), ((), ())), preferred_element_type=jnp.float32
    )


def body(
    hidden,
    cotangent,
    norm_weight,
    gate_in,
    value_in,
    state_in,
    step_in,
    value_kernel,
    value_offset,
    state_kernel,
    state_offset,
    step_bias,
    log_decay,
    skip_weight,
    gated_norm,
    out_weight,
):
    inner_width = HEADS * HEAD_DIM
    row_scale = lax.rsqrt(jnp.mean(hidden * hidden, axis=-1, keepdims=True) + EPSILON)
    normed = (hidden * row_scale * norm_weight).astype(jnp.bfloat16)
    gate_raw = jnp.dot(normed, gate_in, preferred_element_type=jnp.float32)
    value_raw = jnp.dot(normed, value_in, preferred_element_type=jnp.float32)
    step_raw = jnp.dot(normed, step_in, preferred_element_type=jnp.float32)
    state_raw = jnp.dot(normed, state_in, preferred_element_type=jnp.float32)
    state_inputs, state_pullback = jax.vjp(state_branch, state_raw, state_kernel, state_offset)
    mix_args = (
        value_raw,
        step_raw,
        gate_raw,
        state_inputs,
        value_kernel,
        value_offset,
        step_bias,
        log_decay,
        skip_weight,
    )
    gated_rows, mix_pullback = jax.vjp(mix_heads, *mix_args)
    local_squares = jnp.sum(gated_rows * gated_rows, axis=-1, keepdims=True)
    all_squares = lax.psum(local_squares, "tensor")
    gate_scale = lax.rsqrt(all_squares / inner_width + EPSILON)
    scaled = (gated_rows * gate_scale * gated_norm).astype(jnp.bfloat16)
    partial_out = jnp.dot(scaled, out_weight, preferred_element_type=jnp.float32)
    block_out = hidden + lax.psum(partial_out, "tensor")
    upstream = cotangent.astype(jnp.bfloat16)
    grad_out_weight = transposed_left(scaled, upstream)
    grad_scaled = transposed_right(upstream, out_weight)
    grad_gated_norm = jnp.sum(grad_scaled * gated_rows * gate_scale, axis=0)
    weighted = grad_scaled * gated_norm
    local_terms = jnp.sum(weighted * gated_rows, axis=-1, keepdims=True)
    all_terms = lax.psum(local_terms, "tensor")
    grad_gated = weighted * gate_scale - gated_rows * (all_terms * gate_scale**3 / inner_width)
    mix_grads = mix_pullback(grad_gated)
    (
        grad_value_raw,
        grad_step_raw,
        grad_gate_raw,
        grad_state_inputs,
        grad_value_kernel,
        grad_value_offset,
        grad_step_bias,
        grad_log_decay,
        grad_skip_weight,
    ) = mix_grads
    summed_state = lax.psum(grad_state_inputs, "tensor")
    grad_state_raw, grad_state_kernel, grad_state_offset = state_pullback(summed_state)
    gate_low = grad_gate_raw.astype(jnp.bfloat16)
    value_low = grad_value_raw.astype(jnp.bfloat16)
    step_low = grad_step_raw.astype(jnp.bfloat16)
    state_low = grad_state_raw.astype(jnp.bfloat16)
    grad_gate_in = transposed_left(normed, gate_low)
    grad_value_in = transposed_left(normed, value_low)
    grad_step_in = transposed_left(normed, step_low)
    partial_input = (
        transposed_right(gate_low, gate_in)
        + transposed_right(value_low, value_in)
        + transposed_right(step_low, step_in)
    )
    grad_state_in = transposed_left(normed, state_low)
    grad_input = lax.psum(partial_input, "tensor")
    grad_input = grad_input + transposed_right(state_low, state_in)
    norm_product = grad_input * norm_weight
    grad_norm_weight = jnp.sum(grad_input * hidden * row_scale, axis=0)
    row_terms = jnp.sum(norm_product * hidden, axis=-1, keepdims=True)
    grad_hidden = (
        cotangent + norm_product * row_scale - hidden * (row_terms * row_scale**3 / hidden.shape[1])
    )
    (
        grad_norm_weight,
        grad_gate_in,
        grad_value_in,
        grad_state_in,
        grad_step_in,
        grad_value_kernel,
        grad_value_offset,
        grad_state_kernel,
        grad_state_offset,
        grad_step_bias,
        grad_log_decay,
        grad_skip_weight,
        grad_gated_norm,
        grad_out_weight,
    ) = lax.psum(
        (
            grad_norm_weight,
            grad_gate_in,
            grad_value_in,
            grad_state_in,
            grad_step_in,
            grad_value_kernel,
            grad_value_offset,
            grad_state_kernel,
            grad_state_offset,
            grad_step_bias,
            grad_log_decay,
            grad_skip_weight,
            grad_gated_norm,
            grad_out_weight,
        ),
        "dp",
    )
    return (
        block_out,
        grad_hidden,
        grad_norm_weight,
        grad_gate_in,
        grad_value_in,
        grad_state_in,
        grad_step_in,
        grad_value_kernel,
        grad_value_offset,
        grad_state_kernel,
        grad_state_offset,
        grad_step_bias,
        grad_log_decay,
        grad_skip_weight,
        grad_gated_norm,
        grad_out_weight,
    )


def solution(mesh):
    in_specs = (
        P("dp", None),
        P("dp", None),
        P(),
        P(None, "tensor"),
        P(None, "tensor"),
        P(),
        P(None, "tensor"),
        P(None, "tensor"),
        P("tensor"),
        P(),
        P(),
        P("tensor"),
        P("tensor"),
        P("tensor"),
        P("tensor"),
        P("tensor", None),
    )
    out_specs = (
        P("dp", None),
        P("dp", None),
        P(),
        P(None, "tensor"),
        P(None, "tensor"),
        P(),
        P(None, "tensor"),
        P(None, "tensor"),
        P("tensor"),
        P(),
        P(),
        P("tensor"),
        P("tensor"),
        P("tensor"),
        P("tensor"),
        P("tensor", None),
    )
    return jax.shard_map(body, mesh=mesh, in_specs=in_specs, out_specs=out_specs, check_vma=False)
```

profile of v0, /device:TPU:1, one launch (start us, length us, event | category | flops | bytes accessed | tf_op | source)
XLA Modules:
  0.0 812.7 jit_solution(16403970839222383380)
XLA Ops:
  23.4 7.5 fusion.123
  37.6 16.2 %fusion.30 = (f32[4,512,768]{1,2,0:T(8,128)}, f32[4,512,768]{1,2,0:T(8,128)}) fusion(f32[4,512,768]{1,2,0:T(8,128)} %copy.246, f32[768]{0:T(1024)S(1)} %get-tuple-element.338, f32[768]{0:T(1024)S(1)} %get-tuple-element.339, f32[768]{0:T(1024)S(1)} %get-tuple-element.337, f32[768]{0:T(1024)S(1)} %get-tuple-element.336, f32[768]{0:T(1024)S(1)} %copy-done.63), kind=kLoop, calls=%fused_computation.70 | loop fusion | flops 18874368 | bytes 18889728 | tf_op jit(solution)/shard_map/jvp(jit(silu))/mul | solution.py:24
  53.8 8.2 %reshape.223 = f32[4,2,256,12,64]{2,1,4,3,0:T(2,128)} reshape(f32[4,512,768]{1,2,0:T(8,128)} %get-tuple-element.389) | data formatting | bytes 12582912 | tf_op jit(solution)/shard_map/jvp()/reshape | solution.py:76
  77.0 9.8 %fusion.72 = f32[2,4,12,64,128]{4,3,2,0,1:T(8,128)} fusion(f32[4,2,256,128,1]{3,2,4,1,0:T(8,128)} %bitcast.215, f32[4,2,256,12,64]{2,1,4,3,0:T(2,128)} %reshape.223, f32[4,2,256,12]{2,3,1,0:T(8,128)S(1)} %get-tuple-element.413), kind=kOutput, calls=%fused_computation.126 | convolution fusion | flops 2417491968 | bytes 10584064 | tf_op jit(solution)/shard_map/jvp(vmap(bjh,bjhp,bjn->bhpn))/dot_general | solution.py:38
  94.8 7.3 fusion.57
  105.4 31.6 %bitcast_add_fusion.3 = f32[4,2,256,12,64]{2,4,3,1,0:T(8,128)} fusion(f32[4,2,256,12,64]{2,4,3,1,0:T(8,128)S(1)} %fusion.57, f32[4,2,256,12]{2,3,1,0:T(8,128)S(1)} %get-tuple-element.412, f32[4,2,256,12]{2,3,1,0:T(8,128)S(1)} %copy-done.35, f32[4,2,256,12]{2,3,1,0:T(8,128)S(1)} %bitcast.229, f32[4,2,256,256]{3,2,1,0:T(8,128)S(1)} %fusion.125, ...), kind=kOutput, calls=%fused_computation.50 | convolution fusion | flops 4860149760 | bytes 21331968 | tf_op jit(solution)/shard_map/jvp(vmap(bijh,bjhp->bihp))/dot_general | solution.py:36
  137.0 10.4 %copy.262 = f32[4,2,256,12,64]{2,1,0,4,3:T(2,128)} copy(f32[4,2,256,12,64]{2,4,3,1,0:T(8,128)} %bitcast_add_fusion.3) | data formatting | bytes 12582912 | tf_op jit(solution)/shard_map/jvp(vmap())/add | solution.py:53
  147.3 9.0 %reshape.230 = f32[2048,768]{0,1:T(8,128)} reshape(f32[4,2,256,12,64]{2,1,0,4,3:T(2,128)} %copy.262) | data formatting | bytes 12582912 | tf_op jit(solution)/shard_map/jvp()/reshape | solution.py:84
  163.2 11.3 %multiply_reduce_fusion.12 = (f32[2048]{0:T(1024)S(1)}, f32[2048,768]{1,0:T(8,128)}, f32[2048,768]{1,0:T(8,128)}) fusion(f32[2048,768]{1,0:T(8,128)} %copy.264, f32[768]{0:T(1024)S(1)} %mul.547, f32[4,512,768]{2,1,0:T(8,128)} %copy.263, bf16[2048,768]{1,0:T(8,128)(2,1)} %copy-done.3, bf16[768,768]{1,0:T(8,128)(2,1)S(1)} %copy-done), kind=kOutput, calls=%fused_computation.66 | convolution fusion | flops 2430072832 | bytes 29502464 | tf_op jit(solution)/shard_map/dot_general | solution.py:125
  176.9 11.5 %multiply_reduce_fusion.2 = (f32[768]{0:T(1024)}, f32[2048]{0:T(1024)S(1)}, f32[2048,768]{1,0:T(8,128)}) fusion(f32[2048,768]{1,0:T(8,128)} %get-tuple-element.388, f32[2048]{0:T(1024)S(1)} %bitcast.239, f32[768]{0:T(1024)S(1)} %copy-done.53, bf16[768,768]{1,0:T(8,128)(2,1)} %param.35, f32[2048,768]{1,0:T(8,128)} %param.21), kind=kOutput, calls=%fused_computation.52 | convolution fusion | flops 2426926336 | bytes 20076544 | tf_op jit(solution)/shard_map/dot_general | solution.py:99
  191.0 15.7 %fusion.48 = (f32[2048,768]{1,0:T(8,128)}, bf16[2048,768]{1,0:T(8,128)(2,1)}) fusion(f32[2048,768]{1,0:T(8,128)} %get-tuple-element.388, f32[2048]{0:T(1024)S(1)} %bitcast.244, f32[2048]{0:T(1024)S(1)} %bitcast.240, f32[2048,768]{1,0:T(8,128)} %get-tuple-element.422, f32[768]{0:T(1024)S(1)} %copy-done.53, f32[2048,768]{1,0:T(8,128)} %get-tuple-element.421, ...), kind=kLoop, calls=%fused_computation.93 | loop fusion | flops 29884416 | bytes 40916992 | tf_op jit(solution)/shard_map/transpose(jvp())/mul | solution.py:85
  213.3 9.1 %reshape.232 = f32[4,2,256,12,64]{2,1,0,4,3:T(2,128)} reshape(f32[2048,768]{0,1:T(8,128)} %copy.265) | data formatting | bytes 12582912 | tf_op jit(solution)/shard_map/transpose(jvp())/reshape | solution.py:84
  222.4 15.3 %fusion.87 = f32[4,2,256,128]{3,2,1,0:T(8,128)} fusion(f32[2,4,12,64,128]{4,3,2,1,0:T(8,128)} %get-tuple-element.540, f32[4,2,256,12,64]{2,1,0,4,3:T(2,128)} %reshape.232, f32[4,2,256,12]{2,3,1,0:T(8,128)S(1)} %get-tuple-element.412), kind=kOutput, calls=%fused_computation.133 | convolution fusion | flops 2417491968 | bytes 10584064 | tf_op jit(solution)/shard_map/transpose(jvp(vmap(bin,bhpn->bihp)))/dot_general | solution.py:50
  237.8 8.8 %fusion.75 = f32[2,4,12,64,128]{4,3,2,0,1:T(8,128)} fusion(f32[4,2,256,128,1]{3,2,4,1,0:T(8,128)S(1)} %bitcast.213, f32[4,2,256,12,64]{2,1,0,4,3:T(2,128)S(1)} %copy-done.2, f32[4,2,256,12]{2,3,1,0:T(8,128)S(1)} %get-tuple-element.412), kind=kOutput, calls=%fused_computation.127 | convolution fusion | flops 2417491968 | bytes 10584064 | tf_op jit(solution)/shard_map/transpose(jvp(vmap(bin,bhpn->bihp)))/dot_general | solution.py:50
  248.8 7.4 while.35
  256.2 15.5 %fusion.82 = f32[4,2,256,128]{3,2,1,0:T(8,128)} fusion(f32[4,2,256,12,64]{2,1,4,3,0:T(2,128)} %reshape.223, f32[4,2,256,12]{2,3,1,0:T(8,128)S(1)} %get-tuple-element.413, f32[2,4,12,64,128]{4,3,2,1,0:T(8,128)} %get-tuple-element.193), kind=kOutput, calls=%fused_computation.132 | convolution fusion | flops 2417491968 | bytes 10584064 | tf_op jit(solution)/shard_map/transpose(jvp(vmap(bjh,bjhp,bjn->bhpn)))/dot_general | solution.py:38
  278.7 7.2 multiply_reduce_fusion.10
  286.0 41.0 %fusion.9 = (f32[4,2,256,12]{2,3,1,0:T(8,128)S(1)}, f32[4,2,256,12]{2,3,1,0:T(8,128)}, f32[4,2,256,12]{2,3,1,0:T(8,128)}, f32[4,2,256,256]{3,2,1,0:T(8,128)S(1)}) fusion(f32[4,2,256,12]{2,3,1,0:T(8,128)S(1)} %copy-done.35, f32[4,2,256,12]{2,3,1,0:T(8,128)S(1)} %bitcast.230, f32[4,2,256,256]{3,2,1,0:T(8,128)S(1)} %copy-done.25, ...), kind=kOutput, calls=%fused_computation.20 | convolution fusion | flops 4913029120 | bytes 17334272 | tf_op jit(solution)/shard_map/transpose(jvp(vmap(bijh,bjhp->bihp)))/dot_general | solution.py:36
  327.0 13.4 %multiply_reduce_fusion.1 = f32[4,2,256,12]{2,1,3,0:T(2,128)S(1)} fusion(f32[4,2,256,12,64]{2,1,4,3,0:T(2,128)} %reshape.223, f32[4,2,256,12,64]{2,4,3,1,0:T(8,128)} %fusion.54), kind=kLoop, calls=%fused_computation.51 | loop fusion | flops 3121152 | bytes 12681216
  340.4 27.0 %bitcast_add_fusion.2 = f32[4,2,256,12,64]{2,4,3,1,0:T(8,128)} fusion(f32[4,2,256,12,64]{2,4,3,1,0:T(8,128)} %fusion.54, f32[4,2,256,12,64]{2,1,0,4,3:T(2,128)} %reshape.232, f32[12]{0:T(128)S(1)} %copy-done.70, f32[4,2,256,12]{2,3,1,0:T(8,128)S(1)} %get-tuple-element.413, f32[4,2,256,12]{2,3,1,0:T(8,128)S(1)} %copy-done.35, ...), kind=kOutput, calls=%fused_computation.47 | convolution fusion | flops 4863295488 | bytes 27623472 | tf_op jit(solution)/shard_map/transpose(jvp(vmap(bijh,bjhp->bihp)))/dot_general | solution.py:36
  367.4 8.3 %fusion.115 = f32[2048,768]{1,0:T(8,128)} fusion(bf16[768,768]{1,0:T(8,128)(2,1)S(1)} %copy-done.28, f32[2048,768]{1,0:T(8,128)} %get-tuple-element.388, f32[768]{0:T(1024)S(1)} %copy-done.53, f32[2048]{0:T(1024)S(1)} %bitcast.241), kind=kOutput, calls=%fused_computation.192 | convolution fusion | flops 2420637696 | bytes 13773824 | tf_op jit(solution)/shard_map/dot_general | solution.py:146
  384.3 20.0 %reduce-window.16 = f32[4,2,12,2,128]{4,2,3,1,0:T(8,128)S(1)} reduce-window(f32[4,2,12,2,128]{4,2,3,1,0:T(8,128)S(1)} %copy.283, f32[]{:T(128)} %constant.97.clone.1), window={size=1x1x1x1x128 pad=0_0x0_0x0_0x0_0x0_127}, to_apply=%region_18.19 | reduce-window | flops 3121152 | bytes 196612 | tf_op jit(solution)/shard_map/reduce-window.2
  406.1 11.0 %copy.271 = f32[4,2,256,12,64]{2,1,4,3,0:T(2,128)} copy(f32[4,2,256,12,64]{2,4,3,1,0:T(8,128)} %bitcast_add_fusion.2) | data formatting | bytes 12582912 | tf_op jit(solution)/shard_map/transpose(jvp(vmap(bijh,bjhp->bihp)))/add_any | solution.py:36
  417.1 9.0 %reshape.233 = f32[4,512,768]{1,2,0:T(8,128)} reshape(f32[4,2,256,12,64]{2,1,4,3,0:T(2,128)} %copy.271) | data formatting | bytes 12582912 | tf_op jit(solution)/shard_map/transpose(jvp())/reshape | solution.py:76
  432.7 19.1 %multiply_reduce_fusion.7 = (f32[768]{0:T(1024)S(1)}, f32[768]{0:T(1024)S(1)}, f32[768]{0:T(1024)S(1)}, f32[768]{0:T(1024)S(1)}, f32[768]{0:T(1024)S(1)}, /*index=5*/f32[4,512,768]{1,2,0:T(8,128)}, f32[768]{0:T(1024)S(1)}) fusion(f32[4,512,768]{1,2,0:T(8,128)} %copy.246, f32[4,512,768]{1,2,0:T(8,128)} %get-tuple-element.390, f32[4,512,768]{1,2,0:T(8,128)} %reshape.233, ...), kind=kLoop, calls=%fused_computation.57 | loop fusion | flops 33025536 | bytes 31475712 | tf_op jit(solution)/shard_map/transpose(jvp())/reduce_sum | solution.py:23
  457.4 8.6 %fusion.27 = bf16[4,512,768]{1,2,0:T(8,128)(2,1)} fusion(f32[4,512,768]{1,2,0:T(8,128)S(1)} %get-tuple-element.401, f32[4,512,768]{1,2,0:T(8,128)S(1)} %get-tuple-element.402, f32[4,512,768]{1,2,0:T(8,128)} %get-tuple-element.403, f32[4,512,768]{1,2,0:T(8,128)S(1)} %get-tuple-element.400), kind=kLoop, calls=%fused_computation.44 | loop fusion | flops 6291456 | bytes 28311552 | tf_op jit(solution)/shard_map/convert.1
  484.0 7.1 fusion.129
  499.7 40.0 %all-reduce.30.cloned.1.call-done = (f32[2048,768]{1,0:T(8,128)}, f32[2048,768]{1,0:T(8,128)}, f32[4,512,256]{2,1,0:T(8,128)}) async-done(((f32[2048,768]{1,0:T(8,128)}, f32[2048,768]{1,0:T(8,128)}, f32[4,512,256]{2,1,0:T(8,128)}), (f32[2048,768]{1,0:T(8,128)}, f32[2048,768]{1,0:T(8,128)}, f32[4,512,256]{2,1,0:T(8,128)})) %all-reduce.30.cloned.1.call-update) | async-done | bytes 14680080 | tf_op jit(solution)/shard_map/psum | solution.py:147
  550.8 7.9 multiply_reduce_fusion.8
  558.8 70.2 %all-reduce.22 = (f32[768]{0:T(1024)}, f32[768,12]{0,1:T(8,128)}, f32[4,768]{1,0:T(4,128)}, f32[768]{0:T(1024)}, f32[4,256]{1,0:T(4,128)}, /*index=5*/f32[256]{0...) all-reduce(f32[768]{0:T(1024)S(1)} %get-tuple-element.328, ...), channel_id=1, replica_groups=mesh['dp'=16,'tensor'=2] {'dp'}, use_global_device_ids=true, to_apply=%region_25.26 | all-reduce | flops 15908 | bytes 127264 | tf_op jit(solution)/shard_map/psum | solution.py:206
  629.0 14.8 %multiply_subtract_fusion = (f32[2048,768]{1,0:T(8,128)}, f32[2048,768]{1,0:T(8,128)}) fusion(f32[2048,768]{1,0:T(8,128)} %param.20, f32[2048,768]{1,0:T(8,128)} %param.21, f32[2048,768]{1,0:T(8,128)} %get-tuple-element.423, f32[2048]{0:T(1024)S(1)} %fusion.105, f32[768]{0:T(1024)S(1)} %copy-done.51, f32[2048]{0:T(1024)S(1)} %copy-done.34, ...), kind=kLoop, calls=%fused_computation.59 | loop fusion | flops 9437184 | bytes 37768192 | tf_op jit(solution)/shard_map/sub | solution.py:189
  643.8 154.5 %all-reduce.28.cloned.1.call-done = (f32[768,768]{1,0:T(8,128)}, f32[768,768]{1,0:T(8,128)}, f32[768,256]{1,0:T(8,128)}, f32[768,768]{1,0:T(8,128)}) async-done(((f32[768,768]{1,0:T(8,128)}, f32[768,768]{1,0:T(8,128)}, f32[768,256]{1,0:T(8,128)}, f32[768,768]{1,0:T(8,128)}), (f32[768,768]{1,0:T(8,128)}, f32[768,768]{1,0:T(8,128)}, f32[768,256]{1,0:T(8,128)}, ...) | async-done | bytes 7864336 | tf_op jit(solution)/shard_map/psum | solution.py:206
  (283 shorter events, 156.8 us)
Async XLA Ops:
  7.2 156.0 %copy-start = (bf16[768,768]{1,0:T(8,128)(2,1)S(1)}, bf16[768,768]{1,0:T(8,128)(2,1)}, u32[]{:S(2)}) copy-start(bf16[768,768]{1,0:T(8,128)(2,1)} %param.23) | copy-start | bytes 3538948
  7.2 532.6 %all-reduce.30.cloned.1.call-start = ((), (), s32[]{:S(2)}) async-start(), calls=%async_computation.1 | async-start | bytes 29360128 | tf_op jit(solution)/shard_map/psum | solution.py:147
  37.5 16.3 %copy-start.42 = (f32[768]{0:T(1024)}, f32[768]{0:T(1024)S(1)}, u32[]{:S(2)}) copy-start(f32[768]{0:T(1024)S(1)} %get-tuple-element.336) | copy-start | bytes 9220
  37.6 16.3 %copy-start.44 = (f32[768]{0:T(1024)}, f32[768]{0:T(1024)S(1)}, u32[]{:S(2)}) copy-start(f32[768]{0:T(1024)S(1)} %get-tuple-element.337) | copy-start | bytes 9220
  37.6 16.2 %copy-start.46 = (f32[768]{0:T(1024)}, f32[768]{0:T(1024)S(1)}, u32[]{:S(2)}) copy-start(f32[768]{0:T(1024)S(1)} %get-tuple-element.338) | copy-start | bytes 9220
  37.6 16.2 %copy-start.48 = (f32[768]{0:T(1024)}, f32[768]{0:T(1024)S(1)}, u32[]{:S(2)}) copy-start(f32[768]{0:T(1024)S(1)} %get-tuple-element.339) | copy-start | bytes 9220
  71.6 15.2 %copy-start.55 = (f32[1,256]{1,0:T(1,128)}, f32[1,256]{1,0:T(1,128)S(1)}, u32[]{:S(2)}) copy-start(f32[1,256]{1,0:T(1,128)S(1)} %get-tuple-element.415) | copy-start | bytes 3076
  71.6 15.2 %copy-start.57 = (f32[1,256]{1,0:T(1,128)}, f32[1,256]{1,0:T(1,128)S(1)}, u32[]{:S(2)}) copy-start(f32[1,256]{1,0:T(1,128)S(1)} %get-tuple-element.416) | copy-start | bytes 3076
  71.6 15.2 %copy-start.59 = (f32[1,256]{1,0:T(1,128)}, f32[1,256]{1,0:T(1,128)S(1)}, u32[]{:S(2)}) copy-start(f32[1,256]{1,0:T(1,128)S(1)} %get-tuple-element.417) | copy-start | bytes 3076
  71.6 15.2 %copy-start.61 = (f32[1,256]{1,0:T(1,128)}, f32[1,256]{1,0:T(1,128)S(1)}, u32[]{:S(2)}) copy-start(f32[1,256]{1,0:T(1,128)S(1)} %get-tuple-element.418) | copy-start | bytes 3076
  163.2 13.8 %copy-start.53 = (f32[768]{0:T(1024)S(1)}, f32[768]{0:T(1024)}, u32[]{:S(2)}) copy-start(f32[768]{0:T(1024)} %param.34) | copy-start | bytes 9220
  222.4 15.3 %copy-start.2 = (f32[4,2,256,12,64]{2,1,0,4,3:T(2,128)S(1)}, f32[4,2,256,12,64]{2,1,0,4,3:T(2,128)}, u32[]{:S(2)}) copy-start(f32[4,2,256,12,64]{2,1,0,4,3:T(2,128)} %reshape.232) | copy-start | bytes 18874372
  256.2 15.5 %copy-start.9 = (f32[2,4,12,64,128]{4,3,2,1,0:T(8,128)S(1)}, f32[2,4,12,64,128]{4,3,2,1,0:T(8,128)}, u32[]{:S(2)}) copy-start(f32[2,4,12,64,128]{4,3,2,1,0:T(8,128)} %get-tuple-element.193) | copy-start | bytes 9437188
  256.2 15.5 %copy-start.13 = (f32[4,512,128]{2,1,0:T(8,128)S(1)}, f32[4,512,128]{2,1,0:T(8,128)}, u32[]{:S(2)}) copy-start(f32[4,512,128]{2,1,0:T(8,128)} %get-tuple-element.408) | copy-start | bytes 3145732
  271.7 14.2 %slice-start = ((s8[6291456]{0:T(1024)(128)(4,1)}), s8[4194304]{0:T(1024)(128)(4,1)S(1)}, s32[]{:S(2)}) async-start(s8[6291456]{0:T(1024)(128)(4,1)} %bitcast.202), calls=%async_computation.2 | async-start | bytes 8388608
  271.7 14.2 %slice-start.2 = ((s8[6291456]{0:T(1024)(128)(4,1)}), s8[4194304]{0:T(1024)(128)(4,1)S(1)}, s32[]{:S(2)}) async-start(s8[6291456]{0:T(1024)(128)(4,1)} %bitcast.205), calls=%async_computation.4 | async-start | bytes 8388608
  327.0 13.4 %copy-start.70 = (f32[12]{0:T(128)S(1)}, f32[12]{0:T(128)}, u32[]{:S(2)}) copy-start(f32[12]{0:T(128)} %param.33) | copy-start | bytes 148
  340.4 27.0 %copy-start.28 = (bf16[768,768]{1,0:T(8,128)(2,1)S(1)}, bf16[768,768]{1,0:T(8,128)(2,1)}, u32[]{:S(2)}) copy-start(bf16[768,768]{1,0:T(8,128)(2,1)} %param.35) | copy-start | bytes 3538948
  367.3 11.3 %copy-start.11 = (f32[4,512,128]{2,1,0:T(8,128)S(1)}, f32[4,512,128]{2,1,0:T(8,128)}, u32[]{:S(2)}) copy-start(f32[4,512,128]{2,1,0:T(8,128)} %get-tuple-element.409) | copy-start | bytes 3145732
  375.6 29.2 %copy-start.67 = (f32[12]{0:T(128)S(1)}, f32[12]{0:T(128)}, u32[]{:S(2)}) copy-start(f32[12]{0:T(128)} %copy-done.66) | copy-start | bytes 148
  432.7 19.1 %copy-start.43 = (f32[768]{0:T(1024)S(1)}, f32[768]{0:T(1024)}, u32[]{:S(2)}) copy-start(f32[768]{0:T(1024)} %copy-done.42) | copy-start | bytes 9220
  432.7 19.1 %copy-start.45 = (f32[768]{0:T(1024)S(1)}, f32[768]{0:T(1024)}, u32[]{:S(2)}) copy-start(f32[768]{0:T(1024)} %copy-done.44) | copy-start | bytes 9220
  432.7 19.1 %copy-start.47 = (f32[768]{0:T(1024)S(1)}, f32[768]{0:T(1024)}, u32[]{:S(2)}) copy-start(f32[768]{0:T(1024)} %copy-done.46) | copy-start | bytes 9220
  432.7 19.2 %copy-start.49 = (f32[768]{0:T(1024)S(1)}, f32[768]{0:T(1024)}, u32[]{:S(2)}) copy-start(f32[768]{0:T(1024)} %copy-done.48) | copy-start | bytes 9220
  483.6 314.7 %all-reduce.28.cloned.1.call-start = ((), (), s32[]{:S(2)}) async-start(), calls=%async_computation | async-start | bytes 15728640 | tf_op jit(solution)/shard_map/psum | solution.py:206
  484.0 11.3 %slice-start.4 = ((s8[6291456]{0:T(1024)(128)(4,1)}), s8[4194304]{0:T(1024)(128)(4,1)S(1)}, s32[]{:S(2)}) async-start(s8[6291456]{0:T(1024)(128)(4,1)} %bitcast.219), calls=%async_computation.6 | async-start | bytes 8388608
  495.3 44.5 %copy-start.7 = (f32[2048,256]{1,0:T(8,128)S(1)}, f32[2048,256]{1,0:T(8,128)}, u32[]{:S(2)}) copy-start(f32[2048,256]{1,0:T(8,128)} %copy-done.6) | copy-start | bytes 6291460
  499.7 43.7 %copy-start.56 = (f32[1,256]{1,0:T(1,128)S(1)}, f32[1,256]{1,0:T(1,128)}, u32[]{:S(2)}) copy-start(f32[1,256]{1,0:T(1,128)} %copy-done.55) | copy-start | bytes 3076
  499.7 43.7 %copy-start.58 = (f32[1,256]{1,0:T(1,128)S(1)}, f32[1,256]{1,0:T(1,128)}, u32[]{:S(2)}) copy-start(f32[1,256]{1,0:T(1,128)} %copy-done.57) | copy-start | bytes 3076
  499.7 43.7 %copy-start.60 = (f32[1,256]{1,0:T(1,128)S(1)}, f32[1,256]{1,0:T(1,128)}, u32[]{:S(2)}) copy-start(f32[1,256]{1,0:T(1,128)} %copy-done.59) | copy-start | bytes 3076
  499.7 43.7 %copy-start.62 = (f32[1,256]{1,0:T(1,128)S(1)}, f32[1,256]{1,0:T(1,128)}, u32[]{:S(2)}) copy-start(f32[1,256]{1,0:T(1,128)} %copy-done.61) | copy-start | bytes 3076
  550.8 78.1 %copy-start.40 = (f32[2048]{0:T(1024)S(1)}, f32[2048]{0:T(1024)}, u32[]{:S(2)}) copy-start(f32[2048]{0:T(1024)} %copy-done.39) | copy-start | bytes 24580
  (52 other events, 272.6 us)
Sparse Core Ops, SparseCore 0:
  483.8 55.9 all-reduce.29
  548.2 250.0 all-reduce.27
where the time goes:
time: 823 us; the launch traced here: 813 us
  matrix products  255 us (31%)
  waiting for transfers between devices  195 us (24%)
  other arithmetic  155 us (19%)
  local copies, waits for them, and re-layouts  117 us (14%)
  blocking collectives  75.2 us (9%)
  between operations  15.6 us (2%)
    psum x1, waiting for transfers between devices, body(): lax.psum((grad_norm_weight, grad_gate_in, grad_value_in, grad_state_in, g...  155 us
    dot_general x3, matrix products, state_scan(): within = jnp.einsum('bijh,bjhp->bihp', mixing, values, precision=HIGHEST)  99.5 us
    psum x1, blocking collectives, body(): lax.psum((grad_norm_weight, grad_gate_in, grad_value_in, grad_state_in, g...  70.2 us
    psum x1, waiting for transfers between devices, body(): block_out = hidden + lax.psum(partial_out, 'tensor')  40 us
    another operation x9, other arithmetic  34.2 us
    dot_general x3, matrix products, state_scan(): jnp.einsum('bjh,bjhp,bjn->bhpn', tail_decay, values, write_rows, precisio...  32.3 us
    dot_general x3, matrix products, state_scan(): jnp.einsum('bin,bhpn->bihp', read_rows, entering, precision=HIGHEST)  31.4 us
    dot_general x5, matrix products, transposed_right(): lax.dot_general(left_side, right_side, (((1,), (1,)), ((), ())), preferre...  30.5 us
  transfers between devices with their start and end apart: 2, of which 2 were waited for; matrix products, arithmetic and copies ran while one was open for 5% of the time, Pallas kernels for 0%

commit v1 on v0

v1 whole, which is shorter than its diff:
```python
import functools

import jax
import jax.numpy as jnp
from jax import lax
from jax.experimental import pallas as pl
from jax.experimental.pallas import tpu as pltpu
from jax.sharding import PartitionSpec as P

HEAD_DIM = 64
STATE = 128
LENGTH = 512
STRIP = 128
WIDTH = 256
GROUP_HEADS = WIDTH // HEAD_DIM
EPSILON = 1e-05
F32 = jnp.float32
BF16 = jnp.bfloat16
MIB = 1 << 20


def dot_nn(left, right):
    return lax.dot_general(left, right, (((1,), (0,)), ((), ())), preferred_element_type=F32)


def dot_nt(left, right):
    return lax.dot_general(left, right, (((1,), (1,)), ((), ())), preferred_element_type=F32)


def dot_tn(left, right):
    return lax.dot_general(left, right, (((0,), (0,)), ((), ())), preferred_element_type=F32)


def split2(value):
    high = value.astype(BF16)
    return high, (value - high.astype(F32)).astype(BF16)


def split3(value):
    high = value.astype(BF16)
    rest = value - high.astype(F32)
    middle = rest.astype(BF16)
    return high, middle, (rest - middle.astype(F32)).astype(BF16)


def dot3(dot, left, right):
    left_high, left_low = split2(left)
    right_high, right_low = split2(right)
    return dot(left_high, right_high) + (dot(left_high, right_low) + dot(left_low, right_high))


def sigmoid(value):
    return 1.0 / (1.0 + jnp.exp(-value))


def softplus(value):
    return jnp.maximum(value, 0.0) + jnp.log1p(jnp.exp(-jnp.abs(value)))


def triangular(rows, keep_lower):
    down = lax.broadcasted_iota(jnp.int32, (rows, rows), 0)
    along = lax.broadcasted_iota(jnp.int32, (rows, rows), 1)
    return down >= along if keep_lower else down <= along


def running_sum(value, keep_lower):
    high, middle, low = split3(value)
    packed = (
        high.astype(F32)
        + pltpu.roll(middle.astype(F32), 16, 1)
        + pltpu.roll(low.astype(F32), 32, 1)
    ).astype(BF16)
    ones = jnp.where(triangular(value.shape[0], keep_lower), 1.0, 0.0).astype(BF16)
    sums = dot_nn(ones, packed)
    total = sums + pltpu.roll(sums, 128 - 16, 1) + pltpu.roll(sums, 128 - 32, 1)
    lanes = lax.broadcasted_iota(jnp.int32, total.shape, 1)
    return jnp.where(lanes < 16, total, 0.0)


def spread(columns):
    rows = columns.shape[0]
    lanes = lax.broadcasted_iota(jnp.int32, (rows, 128), 1)
    halves = []
    for pair in range(GROUP_HEADS // 2):
        first = jnp.broadcast_to(columns[:, 2 * pair : 2 * pair + 1], (rows, 128))
        second = jnp.broadcast_to(columns[:, 2 * pair + 1 : 2 * pair + 2], (rows, 128))
        halves.append(jnp.where(lanes < HEAD_DIM, first, second))
    return jnp.concatenate(halves, axis=1)


def head_only(value, head):
    lanes = lax.broadcasted_iota(jnp.int32, value.shape, 1)
    return jnp.where((lanes >= head * HEAD_DIM) & (lanes < (head + 1) * HEAD_DIM), value, 0.0).astype(BF16)


def shifted_down(value, by):
    if by == 0:
        return value
    rows = lax.broadcasted_iota(jnp.int32, value.shape, 0)
    return jnp.where(rows >= by, pltpu.roll(value, by, 0), 0.0)


def shifted_up(value, by):
    if by == 0:
        return value
    count = value.shape[0]
    rows = lax.broadcasted_iota(jnp.int32, value.shape, 0)
    return jnp.where(rows < count - by, pltpu.roll(value, count - by, 0), 0.0)


def convolve(value, kernel, offset):
    taps = kernel.shape[0]
    total = offset + kernel[taps - 1 : taps] * value
    for tap in range(taps - 1):
        total = total + kernel[tap : tap + 1] * shifted_down(value, taps - 1 - tap)
    return total


def convolve_back(grad_out, value, kernel):
    taps = kernel.shape[0]
    grad_in = kernel[taps - 1 : taps] * grad_out
    rows = []
    for tap in range(taps):
        by = taps - 1 - tap
        if by:
            grad_in = grad_in + kernel[tap : tap + 1] * shifted_up(grad_out, by)
        rows.append(jnp.sum(grad_out * shifted_down(value, by), axis=0, keepdims=True))
    rows.append(jnp.sum(grad_out, axis=0, keepdims=True))
    rows.append(jnp.zeros((8 - taps - 1, grad_out.shape[1]), F32))
    return grad_in, jnp.concatenate(rows, axis=0)


def forward_kernel(
    hidden_ref, cotangent_ref, norm_ref, gate_in_ref, value_in_ref, state_in_ref, step_in_ref,
    value_kernel_ref, value_offset_ref, state_kernel_ref, state_offset_ref, heads_ref, skip_ref,
    gated_norm_ref, out_weight_ref,
    normed_ref, state_raw_ref, value_raw_ref, gate_raw_ref, mixed_ref, gated_ref, grad_scaled_ref,
    step_pre_ref, log_ref, sums_ref,
    upstream_s, pair_s, steps_s, log_s, log_t_s, squares_s, terms_s,
):
    group = pl.program_id(1)

    @pl.when(group == 0)
    def _():
        rows = hidden_ref[...]
        scale = lax.rsqrt(jnp.mean(rows * rows, axis=-1, keepdims=True) + EPSILON)
        normed = (rows * scale * norm_ref[...]).astype(BF16)
        normed_ref[...] = normed
        upstream_s[...] = cotangent_ref[...].astype(BF16)
        raw = dot_nn(normed, state_in_ref[...])
        state_raw_ref[...] = raw
        pre = convolve(raw, state_kernel_ref[...], state_offset_ref[...])
        conv = pre * sigmoid(pre)
        pair = dot3(dot_nt, conv[:, STATE:], conv[:, :STATE])
        pair_s[...] = jnp.where(triangular(LENGTH, True), pair, 0.0)
        step_pre = dot_nn(normed, step_in_ref[...]) + heads_ref[0:1, :]
        step_pre_ref[...] = step_pre
        lanes = lax.broadcasted_iota(jnp.int32, step_pre.shape, 1)
        steps = jnp.where(lanes < 12, softplus(step_pre), 0.0)
        log = running_sum(steps * heads_ref[1:2, :], True)
        log_ref[...] = log
        transposed = log.T
        for g in range(steps_s.shape[0]):
            back = (128 - GROUP_HEADS * g) % 128
            steps_s[g] = pltpu.roll(steps, back, 1) if back else steps
            log_s[g] = pltpu.roll(log, back, 1) if back else log
            log_t_s[g] = transposed[GROUP_HEADS * g : GROUP_HEADS * g + 8]
        squares_s[...] = jnp.zeros_like(squares_s)
        terms_s[...] = jnp.zeros_like(terms_s)

    normed = normed_ref[...]
    raw = dot_nn(normed, value_in_ref[...])
    value_raw_ref[...] = raw
    pre = convolve(raw, value_kernel_ref[...], value_offset_ref[...])
    values = pre * sigmoid(pre)
    weighted = values * spread(steps_s[group])
    parts = [head_only(weighted, head) for head in range(GROUP_HEADS)]
    log = log_s[group]
    log_t = log_t_s[group]
    strips = []
    for strip in range(LENGTH // STRIP):
        low, high = strip * STRIP, (strip + 1) * STRIP
        pair = pair_s[low:high, :high]
        weights = []
        for head in range(GROUP_HEADS):
            gap = jnp.minimum(log[low:high, head : head + 1] - log_t[head : head + 1, :high], 0.0)
            weights.append((jnp.exp(gap) * pair).astype(BF16))
        strips.append(
            dot_nn(
                jnp.concatenate(weights, axis=1),
                jnp.concatenate([part[:high] for part in parts], axis=0),
            )
        )
    mixed = jnp.concatenate(strips, axis=0) + skip_ref[...] * values
    mixed_ref[...] = mixed
    gate = dot_nn(normed, gate_in_ref[...])
    gate_raw_ref[...] = gate
    gated = mixed * (gate * sigmoid(gate))
    gated_ref[...] = gated
    grad_scaled = dot_nt(upstream_s[...], out_weight_ref[...])
    grad_scaled_ref[...] = grad_scaled
    squares = gated * gated
    terms = grad_scaled * gated_norm_ref[...] * gated
    squares_s[...] += squares[:, :128] + squares[:, 128:]
    terms_s[...] += terms[:, :128] + terms[:, 128:]

    @pl.when(group == pl.num_programs(1) - 1)
    def _():
        lanes = lax.broadcasted_iota(jnp.int32, (LENGTH, 128), 1)
        both = jnp.where(
            lanes == 0,
            jnp.sum(squares_s[...], axis=1, keepdims=True),
            jnp.where(lanes == 1, jnp.sum(terms_s[...], axis=1, keepdims=True), 0.0),
        )
        sums_ref[...] = both.T[:8]


def const_spec(shape):
    return pl.BlockSpec(shape, lambda *_: (0,) * len(shape))


def run_forward(hidden, cotangent, norm, gate_in, value_in, state_in, step_in, value_kernel, value_offset,
                state_kernel, state_offset, heads, skip, gated_norm, out_weight):
    tokens, width = hidden.shape
    channels = gate_in.shape[1]
    groups = channels // WIDTH
    sequences = tokens // LENGTH
    row = lambda s, g: (s, 0)
    block = lambda s, g: (s, g)
    column = lambda s, g: (0, g)
    wide = jax.ShapeDtypeStruct((tokens, channels), F32)
    narrow = jax.ShapeDtypeStruct((tokens, 128), F32)
    wide_spec = pl.BlockSpec((LENGTH, WIDTH), block)
    narrow_spec = pl.BlockSpec((LENGTH, 128), row)
    return pl.pallas_call(
        forward_kernel,
        grid=(sequences, groups),
        in_specs=[
            pl.BlockSpec((LENGTH, width), row),
            pl.BlockSpec((LENGTH, width), row),
            const_spec((1, width)),
            pl.BlockSpec((width, WIDTH), column),
            pl.BlockSpec((width, WIDTH), column),
            const_spec((width, 2 * STATE)),
            const_spec((width, 128)),
            pl.BlockSpec((value_kernel.shape[0], WIDTH), column),
            pl.BlockSpec((1, WIDTH), column),
            const_spec(state_kernel.shape),
            const_spec((1, 2 * STATE)),
            const_spec((8, 128)),
            pl.BlockSpec((1, WIDTH), column),
            pl.BlockSpec((1, WIDTH), column),
            pl.BlockSpec((WIDTH, width), lambda s, g: (g, 0)),
        ],
        out_specs=[
            pl.BlockSpec((LENGTH, width), row),
            pl.BlockSpec((LENGTH, 2 * STATE), row),
            wide_spec,
            wide_spec,
            wide_spec,
            wide_spec,
            wide_spec,
            narrow_spec,
            narrow_spec,
            pl.BlockSpec((8, LENGTH), lambda s, g: (0, s)),
        ],
        out_shape=[
            jax.ShapeDtypeStruct((tokens, width), BF16),
            jax.ShapeDtypeStruct((tokens, 2 * STATE), F32),
            wide,
            wide,
            wide,
            wide,
            wide,
            narrow,
            narrow,
            jax.ShapeDtypeStruct((8, tokens), F32),
        ],
        scratch_shapes=[
            pltpu.VMEM((LENGTH, width), BF16),
            pltpu.VMEM((LENGTH, LENGTH), F32),
            pltpu.VMEM((groups, LENGTH, 128), F32),
            pltpu.VMEM((groups, LENGTH, 128), F32),
            pltpu.VMEM((groups, 8, LENGTH), F32),
            pltpu.VMEM((LENGTH, 128), F32),
            pltpu.VMEM((LENGTH, 128), F32),
        ],
        compiler_params=pltpu.CompilerParams(vmem_limit_bytes=56 * MIB),
        name="forward_mix",
    )(hidden, cotangent, norm, gate_in, value_in, state_in, step_in, value_kernel, value_offset,
      state_kernel, state_offset, heads, skip, gated_norm, out_weight)


def row_factors(own_ref, other_ref, inner):
    sums = own_ref[...] + other_ref[...]
    columns = jnp.concatenate([sums, jnp.zeros((120, sums.shape[1]), F32)], axis=0).T
    scale = lax.rsqrt(columns[:, 0:1] / inner + EPSILON)
    return scale, columns[:, 1:2] * (scale * scale * scale) / inner


def out_kernel(inner, gated_ref, cotangent_ref, own_ref, other_ref, gated_norm_ref, scaled_ref, grad_ref):
    scale, _ = row_factors(own_ref, other_ref, inner)
    scaled = (gated_ref[...] * scale * gated_norm_ref[...]).astype(BF16)
    scaled_ref[...] = scaled
    grad = dot_tn(scaled, cotangent_ref[...].astype(BF16))

    @pl.when(pl.program_id(0) == 0)
    def _():
        grad_ref[...] = grad

    @pl.when(pl.program_id(0) != 0)
    def _():
        grad_ref[...] += grad


def run_out(gated, cotangent, own, other, gated_norm, inner):
    tokens, channels = gated.shape
    width = cotangent.shape[1]
    row = lambda s: (s, 0)
    return pl.pallas_call(
        functools.partial(out_kernel, inner),
        grid=(tokens // LENGTH,),
        in_specs=[
            pl.BlockSpec((LENGTH, channels), row),
            pl.BlockSpec((LENGTH, width), row),
            pl.BlockSpec((8, LENGTH), lambda s: (0, s)),
            pl.BlockSpec((8, LENGTH), lambda s: (0, s)),
            const_spec((1, channels)),
        ],
        out_specs=[pl.BlockSpec((LENGTH, channels), row), const_spec((channels, width))],
        out_shape=[
            jax.ShapeDtypeStruct((tokens, channels), BF16),
            jax.ShapeDtypeStruct((channels, width), F32),
        ],
        compiler_params=pltpu.CompilerParams(vmem_limit_bytes=56 * MIB),
        name="grad_out_weight",
    )(gated, cotangent, own, other, gated_norm)


def gate_kernel(
    inner, normed_ref, scaled_ref, gated_ref, mixed_ref, gate_ref, grad_scaled_ref, own_ref, other_ref,
    gated_norm_ref, out_weight_ref,
    grad_mixed_ref, gate_low_ref, partial_ref, grad_ref, grad_norm_ref,
):
    first = pl.program_id(0) == 0
    scale, factor = row_factors(own_ref, other_ref, inner)
    normed = normed_ref[...]
    for group in range(gated_ref.shape[1] // WIDTH):
        columns = slice(group * WIDTH, (group + 1) * WIDTH)
        gated = gated_ref[:, columns]
        gate = gate_ref[:, columns]
        scaled_by = grad_scaled_ref[:, columns] * scale
        norm_rows = jnp.sum(scaled_by * gated, axis=0, keepdims=True)
        grad_gated = scaled_by * gated_norm_ref[:, columns] - gated * factor
        s = sigmoid(gate)
        grad_mixed_ref[:, columns] = grad_gated * (gate * s)
        low = (grad_gated * mixed_ref[:, columns] * (s * (1.0 + gate * (1.0 - s)))).astype(BF16)
        gate_low_ref[:, columns] = low
        grad = dot_tn(normed, low)

        @pl.when(first)
        def _():
            grad_ref[:, columns] = grad
            grad_norm_ref[:, columns] = norm_rows

        @pl.when(jnp.logical_not(first))
        def _():
            grad_ref[:, columns] += grad
            grad_norm_ref[:, columns] += norm_rows

    partial_ref[...] = dot_nn(scaled_ref[...], out_weight_ref[...])


def run_gate(normed, scaled, gated, mixed, gate_raw, grad_scaled, own, other, gated_norm, out_weight, inner):
    tokens, channels = gated.shape
    width = normed.shape[1]
    row = lambda s: (s, 0)
    wide = pl.BlockSpec((LENGTH, channels), row)
    return pl.pallas_call(
        functools.partial(gate_kernel, inner),
        grid=(tokens // LENGTH,),
        in_specs=[
            pl.BlockSpec((LENGTH, width), row),
            wide,
            wide,
            wide,
            wide,
            wide,
            pl.BlockSpec((8, LENGTH), lambda s: (0, s)),
            pl.BlockSpec((8, LENGTH), lambda s: (0, s)),
            const_spec((1, channels)),
            const_spec((channels, width)),
        ],
        out_specs=[
            wide,
            wide,
            pl.BlockSpec((LENGTH, width), row),
            const_spec((width, channels)),
            const_spec((1, channels)),
        ],
        out_shape=[
            jax.ShapeDtypeStruct((tokens, channels), F32),
            jax.ShapeDtypeStruct((tokens, channels), BF16),
            jax.ShapeDtypeStruct((tokens, width), F32),
            jax.ShapeDtypeStruct((width, channels), F32),
            jax.ShapeDtypeStruct((1, channels), F32),
        ],
        compiler_params=pltpu.CompilerParams(vmem_limit_bytes=60 * MIB),
        name="grad_gate",
    )(normed, scaled, gated, mixed, gate_raw, grad_scaled, own, other, gated_norm, out_weight)


def scan_back_kernel(
    normed_ref, state_raw_ref, value_raw_ref, grad_mixed_ref, step_pre_ref, log_ref,
    value_kernel_ref, value_offset_ref, state_kernel_ref, state_offset_ref, heads_ref, skip_ref,
    value_low_ref, step_low_ref, grad_state_ref, grad_value_ref, grad_step_ref, rows_ref, head_rows_ref,
    normed_t_s, conv_s, pair_s, grad_pair_s, steps_s, log_s, log_t_s, row_sums_s, column_sums_s, direct_s,
):
    sequence, group = pl.program_id(0), pl.program_id(1)

    @pl.when(group == 0)
    def _():
        normed_t_s[...] = normed_ref[...].T
        raw = state_raw_ref[...]
        pre = convolve(raw, state_kernel_ref[...], state_offset_ref[...])
        conv = pre * sigmoid(pre)
        conv_s[...] = conv
        pair = dot3(dot_nt, conv[:, :STATE], conv[:, STATE:])
        pair_s[...] = jnp.where(triangular(LENGTH, False), pair, 0.0)
        grad_pair_s[...] = jnp.zeros_like(grad_pair_s)
        step_pre = step_pre_ref[...]
        lanes = lax.broadcasted_iota(jnp.int32, step_pre.shape, 1)
        steps = jnp.where(lanes < 12, softplus(step_pre), 0.0)
        log = log_ref[...]
        transposed = log.T
        for g in range(steps_s.shape[0]):
            back = (128 - GROUP_HEADS * g) % 128
            steps_s[g] = pltpu.roll(steps, back, 1) if back else steps
            log_s[g] = pltpu.roll(log, back, 1) if back else log
            log_t_s[g] = transposed[GROUP_HEADS * g : GROUP_HEADS * g + 8]
        column_sums_s[...] = jnp.zeros_like(column_sums_s)
        direct_s[...] = jnp.zeros_like(direct_s)

    raw = value_raw_ref[...]
    kernel = value_kernel_ref[...]
    pre = convolve(raw, kernel, value_offset_ref[...])
    s = sigmoid(pre)
    values = pre * s
    steps = spread(steps_s[group])
    weighted = values * steps
    grad_mixed = grad_mixed_ref[...]
    grad_low = grad_mixed.astype(BF16)
    weighted_parts = [head_only(weighted, head) for head in range(GROUP_HEADS)]
    grad_parts = [head_only(grad_mixed, head) for head in range(GROUP_HEADS)]
    log = log_s[group]
    log_t = log_t_s[group]
    strips = []
    columns = []
    row_sums = [jnp.zeros((1, LENGTH), F32) for _ in range(GROUP_HEADS)]
    for strip in range(LENGTH // STRIP):
        low, high = strip * STRIP, (strip + 1) * STRIP
        pair = pair_s[low:high, low:]
        total = None
        products = []
        sums = []
        for head in range(GROUP_HEADS):
            gap = jnp.minimum(log_t[head : head + 1, low:] - log[low:high, head : head + 1], 0.0)
            decay = jnp.exp(gap)
            weight = decay * pair
            products.append(weight.astype(BF16))
            grad_weight = dot_nt(weighted_parts[head][low:high], grad_low[low:])
            grad_pair = grad_weight * decay
            total = grad_pair if total is None else total + grad_pair
            both = grad_weight * weight
            sums.append(jnp.sum(both, axis=1, keepdims=True))
            along = jnp.sum(both, axis=0, keepdims=True)
            if low:
                along = jnp.concatenate([jnp.zeros((1, low), F32), along], axis=1)
            row_sums[head] = row_sums[head] + along
        grad_pair_s[low:high, low:] += total
        columns.append(sums)
        strips.append(
            dot_nn(
                jnp.concatenate(products, axis=1),
                jnp.concatenate([part[low:] for part in grad_parts], axis=0),
            )
        )
    reached = jnp.concatenate(strips, axis=0)
    row_sums_s[group] = jnp.concatenate(row_sums + [jnp.zeros((8 - GROUP_HEADS, LENGTH), F32)], axis=0)
    lanes = lax.broadcasted_iota(jnp.int32, (LENGTH, 128), 1)
    place = group * GROUP_HEADS
    column_sums = jnp.zeros((LENGTH, 128), F32)
    for head in range(GROUP_HEADS):
        one = jnp.concatenate([sums[head] for sums in columns], axis=0)
        column_sums = jnp.where(lanes == place + head, one, column_sums)
    column_sums_s[...] += column_sums
    down = lax.broadcasted_iota(jnp.int32, (WIDTH, 128), 0)
    across = lax.broadcasted_iota(jnp.int32, (WIDTH, 128), 1)
    start = (across - place) * HEAD_DIM
    picks = jnp.where((down >= start) & (down < start + HEAD_DIM), 1.0, 0.0).astype(BF16)
    direct_high, direct_low = split2(values * reached)
    direct_s[...] += dot_nn(direct_high, picks) + dot_nn(direct_low, picks)

    grad_values = steps * reached + skip_ref[...] * grad_mixed
    grad_pre = grad_values * (s * (1.0 + pre * (1.0 - s)))
    grad_raw, rows = convolve_back(grad_pre, raw, kernel)
    rows = jnp.concatenate([rows[:5], jnp.sum(grad_mixed * values, axis=0, keepdims=True), rows[6:]], axis=0)
    value_low = grad_raw.astype(BF16)
    value_low_ref[...] = value_low
    grad_value = dot_nn(normed_t_s[...], value_low)

    @pl.when(sequence == 0)
    def _():
        grad_value_ref[group] = grad_value
        rows_ref[group] = rows

    @pl.when(sequence != 0)
    def _():
        grad_value_ref[group] += grad_value
        rows_ref[group] += rows

    @pl.when(group == pl.num_programs(1) - 1)
    def _():
        conv = conv_s[...]
        grad_pair = jnp.where(triangular(LENGTH, False), grad_pair_s[...], 0.0)
        grad_write = dot3(dot_nn, grad_pair, conv[:, STATE:])
        grad_read = dot3(dot_tn, grad_pair, conv[:, :STATE])
        grad_state_ref[...] = jnp.concatenate([grad_write, grad_read], axis=1)
        groups = row_sums_s.shape[0]
        row_sums = jnp.concatenate(
            [row_sums_s[g, :GROUP_HEADS] for g in range(groups)]
            + [jnp.zeros((128 - GROUP_HEADS * groups, LENGTH), F32)],
            axis=0,
        ).T
        memory = running_sum(row_sums - column_sums_s[...], False)
        step_pre = step_pre_ref[...]
        rate = heads_ref[1:2, :]
        grad_steps = direct_s[...] + rate * memory
        grad_raw = grad_steps * sigmoid(step_pre)
        grad_raw = jnp.where(lanes < 12, grad_raw, 0.0)
        step_low = grad_raw.astype(BF16)
        step_low_ref[...] = step_low
        grad_step = dot_nn(normed_t_s[...], step_low)
        decay_row = rate * jnp.sum(jnp.where(lanes < 12, softplus(step_pre), 0.0) * memory, axis=0, keepdims=True)
        head_rows = jnp.concatenate(
            [jnp.sum(grad_raw, axis=0, keepdims=True), decay_row, jnp.zeros((6, 128), F32)], axis=0
        )

        @pl.when(sequence == 0)
        def _():
            grad_step_ref[...] = grad_step
            head_rows_ref[...] = head_rows

        @pl.when(sequence != 0)
        def _():
            grad_step_ref[...] += grad_step
            head_rows_ref[...] += head_rows


def run_scan_back(normed, state_raw, value_raw, grad_mixed, step_pre, log, value_kernel, value_offset,
                  state_kernel, state_offset, heads, skip):
    tokens, width = normed.shape
    channels = value_raw.shape[1]
    groups = channels // WIDTH
    row = lambda s, g: (s, 0)
    block = lambda s, g: (s, g)
    column = lambda s, g: (0, g)
    return pl.pallas_call(
        scan_back_kernel,
        grid=(tokens // LENGTH, groups),
        in_specs=[
            pl.BlockSpec((LENGTH, width), row),
            pl.BlockSpec((LENGTH, 2 * STATE), row),
            pl.BlockSpec((LENGTH, WIDTH), block),
            pl.BlockSpec((LENGTH, WIDTH), block),
            pl.BlockSpec((LENGTH, 128), row),
            pl.BlockSpec((LENGTH, 128), row),
            pl.BlockSpec((value_kernel.shape[0], WIDTH), column),
            pl.BlockSpec((1, WIDTH), column),
            const_spec(state_kernel.shape),
            const_spec((1, 2 * STATE)),
            const_spec((8, 128)),
            pl.BlockSpec((1, WIDTH), column),
        ],
        out_specs=[
            pl.BlockSpec((LENGTH, WIDTH), block),
            pl.BlockSpec((LENGTH, 128), row),
            pl.BlockSpec((LENGTH, 2 * STATE), row),
            const_spec((groups, width, WIDTH)),
            const_spec((width, 128)),
            const_spec((groups, 8, WIDTH)),
            const_spec((8, 128)),
        ],
        out_shape=[
            jax.ShapeDtypeStruct((tokens, channels), BF16),
            jax.ShapeDtypeStruct((tokens, 128), BF16),
            jax.ShapeDtypeStruct((tokens, 2 * STATE), F32),
            jax.ShapeDtypeStruct((groups, width, WIDTH), F32),
            jax.ShapeDtypeStruct((width, 128), F32),
            jax.ShapeDtypeStruct((groups, 8, WIDTH), F32),
            jax.ShapeDtypeStruct((8, 128), F32),
        ],
        scratch_shapes=[
            pltpu.VMEM((width, LENGTH), BF16),
            pltpu.VMEM((LENGTH, 2 * STATE), F32),
            pltpu.VMEM((LENGTH, LENGTH), F32),
            pltpu.VMEM((LENGTH, LENGTH), F32),
            pltpu.VMEM((groups, LENGTH, 128), F32),
            pltpu.VMEM((groups, LENGTH, 128), F32),
            pltpu.VMEM((groups, 8, LENGTH), F32),
            pltpu.VMEM((groups, 8, LENGTH), F32),
            pltpu.VMEM((LENGTH, 128), F32),
            pltpu.VMEM((LENGTH, 128), F32),
        ],
        compiler_params=pltpu.CompilerParams(vmem_limit_bytes=60 * MIB),
        name="scan_back",
    )(normed, state_raw, value_raw, grad_mixed, step_pre, log, value_kernel, value_offset, state_kernel,
      state_offset, heads, skip)


def in_kernel(
    core_ref, own_ref, other_ref, state_raw_ref, normed_ref, gate_low_ref, value_low_ref, step_low_ref,
    gate_in_ref, value_in_ref, step_in_ref, state_in_ref, kernel_ref, offset_ref,
    partial_ref, grad_ref, rows_ref,
):
    raw = state_raw_ref[...]
    kernel = kernel_ref[...]
    pre = convolve(raw, kernel, offset_ref[...])
    s = sigmoid(pre)
    grad_pre = (own_ref[...] + other_ref[...]) * (s * (1.0 + pre * (1.0 - s)))
    grad_raw, rows = convolve_back(grad_pre, raw, kernel)
    low = grad_raw.astype(BF16)
    grad = dot_tn(normed_ref[...], low)

    @pl.when(pl.program_id(0) == 0)
    def _():
        grad_ref[...] = grad
        rows_ref[...] = rows

    @pl.when(pl.program_id(0) != 0)
    def _():
        grad_ref[...] += grad
        rows_ref[...] += rows

    partial_ref[...] = (
        dot_nt(gate_low_ref[...], gate_in_ref[...])
        + dot_nt(value_low_ref[...], value_in_ref[...])
        + dot_nt(jnp.concatenate([step_low_ref[...], low], axis=1),
                 jnp.concatenate([step_in_ref[...], state_in_ref[...]], axis=1))
    )


def run_in(core, own, other, state_raw, normed, gate_low, value_low, step_low, gate_in, value_in, step_in,
           state_in, state_kernel, state_offset):
    tokens, width = normed.shape
    channels = value_low.shape[1]
    row = lambda s, c: (s, 0)
    half = lambda s, c: (s, c[0])
    mine = lambda s, c: (0, c[0])
    return pl.pallas_call(
        in_kernel,
        grid_spec=pltpu.PrefetchScalarGridSpec(
            num_scalar_prefetch=1,
            grid=(tokens // LENGTH,),
            in_specs=[
                pl.BlockSpec((LENGTH, STATE), half),
                pl.BlockSpec((LENGTH, STATE), row),
                pl.BlockSpec((LENGTH, STATE), half),
                pl.BlockSpec((LENGTH, width), row),
                pl.BlockSpec((LENGTH, channels), row),
                pl.BlockSpec((LENGTH, channels), row),
                pl.BlockSpec((LENGTH, 128), row),
                const_spec((width, channels)),
                const_spec((width, channels)),
                const_spec((width, 128)),
                pl.BlockSpec((width, STATE), mine),
                pl.BlockSpec((state_kernel.shape[0], STATE), mine),
                pl.BlockSpec((1, STATE), mine),
            ],
            out_specs=[
                pl.BlockSpec((LENGTH, width), row),
                const_spec((width, STATE)),
                const_spec((8, STATE)),
            ],
        ),
        out_shape=[
            jax.ShapeDtypeStruct((tokens, width), F32),
            jax.ShapeDtypeStruct((width, STATE), F32),
            jax.ShapeDtypeStruct((8, STATE), F32),
        ],
        compiler_params=pltpu.CompilerParams(vmem_limit_bytes=60 * MIB),
        name="grad_in",
    )(core, own, other, state_raw, normed, gate_low, value_low, step_low, gate_in, value_in, step_in,
      state_in, state_kernel, state_offset)


def last_kernel(hidden_ref, cotangent_ref, own_ref, other_ref, out_own_ref, out_other_ref, norm_ref,
                block_ref, grad_ref, rows_ref):
    rows = hidden_ref[...]
    block_ref[...] = rows + (out_own_ref[...] + out_other_ref[...])
    scale = lax.rsqrt(jnp.mean(rows * rows, axis=-1, keepdims=True) + EPSILON)
    grad = own_ref[...] + other_ref[...]
    product = grad * norm_ref[...]
    terms = jnp.sum(product * rows, axis=-1, keepdims=True)
    grad_ref[...] = (
        cotangent_ref[...] + product * scale - rows * (terms * (scale * scale * scale) / rows.shape[1])
    )
    norm_rows = jnp.sum(grad * rows * scale, axis=0, keepdims=True)

    @pl.when(pl.program_id(0) == 0)
    def _():
        rows_ref[...] = norm_rows

    @pl.when(pl.program_id(0) != 0)
    def _():
        rows_ref[...] += norm_rows


def run_last(hidden, cotangent, own, other, out_own, out_other, norm):
    tokens, width = hidden.shape
    wide = pl.BlockSpec((LENGTH // 2, width), lambda s: (s, 0))
    return pl.pallas_call(
        last_kernel,
        grid=(2 * tokens // LENGTH,),
        in_specs=[wide] * 6 + [const_spec((1, width))],
        out_specs=[wide, wide, const_spec((1, width))],
        out_shape=[
            jax.ShapeDtypeStruct((tokens, width), F32),
            jax.ShapeDtypeStruct((tokens, width), F32),
            jax.ShapeDtypeStruct((1, width), F32),
        ],
        compiler_params=pltpu.CompilerParams(vmem_limit_bytes=56 * MIB),
        name="grad_hidden",
    )(hidden, cotangent, own, other, out_own, out_other, norm)


SWAP = [(0, 1), (1, 0)]


def swap(value):
    return lax.ppermute(value, "tensor", SWAP)


def body(hidden, cotangent, norm_weight, gate_in, value_in, state_in, step_in, value_kernel, value_offset,
         state_kernel, state_offset, step_bias, log_decay, skip_weight, gated_norm, out_weight):
    core = lax.axis_index("tensor")
    tokens, width = hidden.shape
    channels = gate_in.shape[1]
    heads = step_in.shape[1]
    inner = 2 * channels
    norm = norm_weight.reshape(1, width)
    step_in = jnp.pad(step_in, ((0, 0), (0, 128 - heads)))
    head_rows = jnp.stack([step_bias, -jnp.exp(log_decay)])
    head_rows = jnp.pad(head_rows, ((0, 6), (0, 128 - heads)))
    skip = jnp.repeat(skip_weight, HEAD_DIM).reshape(1, channels)
    value_offset = value_offset.reshape(1, channels)
    state_offset = state_offset.reshape(1, 2 * STATE)
    gated_norm = gated_norm.reshape(1, channels)

    (normed, state_raw, value_raw, gate_raw, mixed, gated, grad_scaled, step_pre, log, sums) = run_forward(
        hidden, cotangent, norm, gate_in, value_in, state_in, step_in, value_kernel, value_offset, state_kernel,
        state_offset, head_rows, skip, gated_norm, out_weight,
    )
    other_sums = swap(sums)
    scaled, grad_out_weight = run_out(gated, cotangent, sums, other_sums, gated_norm, inner)
    grad_mixed, gate_low, partial_out, grad_gate_in, grad_gated_norm = run_gate(
        normed, scaled, gated, mixed, gate_raw, grad_scaled, sums, other_sums, gated_norm, out_weight, inner
    )
    other_out = swap(partial_out)
    value_low, step_low, grad_state, grad_value, grad_step_in, value_rows, grad_heads = run_scan_back(
        normed, state_raw, value_raw, grad_mixed, step_pre, log, value_kernel, value_offset, state_kernel,
        state_offset, head_rows, skip,
    )
    outgoing = jnp.where(core == 0, grad_state[:, STATE:], grad_state[:, :STATE])
    other_state = swap(outgoing)
    core_index = core.astype(jnp.int32).reshape(1)
    partial_in, grad_state_in, state_rows = run_in(
        core_index, grad_state, other_state, state_raw, normed, gate_low, value_low, step_low, gate_in, value_in,
        step_in, state_in, state_kernel, state_offset,
    )
    other_in = swap(partial_in)
    block_out, grad_hidden, grad_norm = run_last(
        hidden, cotangent, partial_in, other_in, partial_out, other_out, norm
    )
    (grad_out_weight, grad_gate_in, grad_value, grad_state_in, grad_step_in, value_rows, state_rows, grad_heads,
     grad_gated_norm, grad_norm) = lax.psum(
        (grad_out_weight, grad_gate_in, grad_value, grad_state_in, grad_step_in, value_rows, state_rows,
         grad_heads, grad_gated_norm, grad_norm), "dp",
    )
    state_all = jnp.concatenate([grad_state_in, state_rows], axis=0)
    state_other = swap(state_all)
    state_all = jnp.where(
        core == 0,
        jnp.concatenate([state_all, state_other], axis=1),
        jnp.concatenate([state_other, state_all], axis=1),
    )
    grad_value_in = jnp.concatenate([grad_value[g] for g in range(grad_value.shape[0])], axis=1)
    value_rows = jnp.concatenate([value_rows[g] for g in range(value_rows.shape[0])], axis=1)
    taps = value_kernel.shape[0]
    return (
        block_out,
        grad_hidden,
        grad_norm.reshape(width),
        grad_gate_in,
        grad_value_in,
        state_all[:width],
        grad_step_in[:, :heads],
        value_rows[:taps],
        value_rows[taps],
        state_all[width : width + taps],
        state_all[width + taps],
        grad_heads[0, :heads],
        grad_heads[1, :heads],
        value_rows[taps + 1].reshape(heads, HEAD_DIM).sum(axis=1),
        grad_gated_norm.reshape(channels),
        grad_out_weight,
    )


def solution(mesh):
    in_specs = (
        P("dp", None),
        P("dp", None),
        P(),
        P(None, "tensor"),
        P(None, "tensor"),
        P(),
        P(None, "tensor"),
        P(None, "tensor"),
        P("tensor"),
        P(),
        P(),
        P("tensor"),
        P("tensor"),
        P("tensor"),
        P("tensor"),
        P("tensor", None),
    )
    out_specs = (
        P("dp", None),
        P("dp", None),
        P(),
        P(None, "tensor"),
        P(None, "tensor"),
        P(),
        P(None, "tensor"),
        P(None, "tensor"),
        P("tensor"),
        P(),
        P(),
        P("tensor"),
        P("tensor"),
        P("tensor"),
        P("tensor"),
        P("tensor", None),
    )
    return jax.shard_map(body, mesh=mesh, in_specs=in_specs, out_specs=out_specs, check_vma=False)
```

time: 823 us -> 444 us (0.54); the launches traced: 813 us -> 444 us
  matrix products: 255 us -> 0 us
  Pallas kernels: 0 us -> 167 us
  other arithmetic: 155 us -> 7.18 us
  local copies, waits for them, and re-layouts: 117 us -> 20.3 us
  waiting for transfers between devices: 195 us -> 165 us
    dot_general x27 -> x0, matrix products: 255 us -> none  [the longest x3 99.5 us: state_scan(): within = jnp.einsum('bijh,bjhp->bihp', mixing, values, precision=HIGHEST)]
    pallas_call x0 -> x6, Pallas kernels: none -> 167 us  [the longest x1 59.7 us: run_scan_back(): pl.pallas_call(scan_back_kernel, grid=(tokens // LENGTH, groups), in_spec...]
    psum x2 -> x1, waiting for transfers between devices: 195 us -> 142 us  [body(): lax.psum((grad_out_weight, grad_gate_in, grad_value, grad_state_in, grad_...]
    reshape x12 -> x3, local copies, waits for them, and re-layouts: 55.8 us -> 3.81 us  [the longest x1 1.27 us: body(): norm = norm_weight.reshape(1, width)]
    mul x6 -> x0, other arithmetic: 40.8 us -> none  [the longest x2 18.8 us: conv_silu(): return jax.nn.silu(summed)]
    reduce_sum x10 -> x1, other arithmetic: 39.6 us -> 0.63 us  [body(): value_rows[taps + 1].reshape(heads, HEAD_DIM).sum(axis=1)]
    another operation x9 -> x2, other arithmetic: 34.2 us -> 1.91 us  [body(): head_rows = jnp.stack([step_bias, -jnp.exp(log_decay)])]
    ppermute x0 -> x5, waiting for transfers between devices: none -> 22.8 us  [swap(): return lax.ppermute(value, 'tensor', SWAP)]
  transfers between devices with their start and end apart: 2 -> 6, of which waited for: 2 -> 5; matrix products, arithmetic and copies ran while one was open for 5% -> 2% of each run, Pallas kernels for 0% -> 4%
where the time goes in v1:
time: 444 us
  Pallas kernels  167 us (38%)
  waiting for transfers between devices  165 us (37%)
  blocking collectives  68.5 us (15%)
  local copies, waits for them, and re-layouts  20.3 us (5%)
  between operations  14.2 us (3%)
  other arithmetic  7.18 us (2%)
    psum x1, waiting for transfers between devices, body(): lax.psum((grad_out_weight, grad_gate_in, grad_value, grad_state_in, grad_...  142 us
    psum x1, blocking collectives, body(): lax.psum((grad_out_weight, grad_gate_in, grad_value, grad_state_in, grad_...  68.5 us
    pallas_call x1, Pallas kernels, run_scan_back(): pl.pallas_call(scan_back_kernel, grid=(tokens // LENGTH, groups), in_spec...  59.7 us
    pallas_call x1, Pallas kernels, run_forward(): pl.pallas_call(forward_kernel, grid=(sequences, groups), in_specs=[pl.Blo...  41.8 us
    ppermute x5, waiting for transfers between devices, swap(): return lax.ppermute(value, 'tensor', SWAP)  22.8 us
    pallas_call x1, Pallas kernels, run_gate(): pl.pallas_call(functools.partial(gate_kernel, inner), grid=(tokens // LEN...  21.7 us
    pallas_call x1, Pallas kernels, run_last(): pl.pallas_call(last_kernel, grid=(2 * tokens // LENGTH,), in_specs=[wide]...  18.3 us
    pallas_call x1, Pallas kernels, run_in(): pl.pallas_call(in_kernel, grid_spec=pltpu.PrefetchScalarGridSpec(num_scal...  15.2 us
  transfers between devices with their start and end apart: 6, of which 5 were waited for; matrix products, arithmetic and copies ran while one was open for 2% of the time, Pallas kernels for 4%

profile of v1, /device:TPU:1, one launch (start us, length us, event | category | flops | bytes accessed | tf_op | source)
XLA Modules:
  0.0 443.6 jit_solution(15363170424579390746)
XLA Ops:
  7.2 1.3 reshape.57.gated_norm_ref
  8.5 0.9 copy.32
  9.4 0.7 broadcast_in_dim.3
  10.8 0.7 negate_bitcast_fusion
  11.5 1.3 reshape.54.norm_ref
  12.7 1.3 reshape.55.value_offset_ref
  14.0 0.7 pad.8.step_in_ref
  14.7 1.3 select_maximum_fusion.heads_ref
  16.0 41.8 %forward_mix.1 = (bf16[2048,768]{1,0:T(8,128)(2,1)}, f32[2048,256]{1,0:T(8,128)}, f32[2048,768]{1,0:T(8,128)}, f32[2048,768]{1,0:T(8,128)}, f32[2048,768]{1,0:T(...) custom-call(f32[2048,768]{1,0:T(8,128)} %hidden_ref.3, ...), custom_call_target="tpu_custom_call" | custom-call | tf_op jit(solution)/shard_map/forward_mix/pallas_call | solution.py:235
  57.8 1.4 collective-permute-done.other_ref
  59.9 10.7 %grad_out_weight.1 = (bf16[2048,768]{1,0:T(8,128)(2,1)}, f32[768,768]{1,0:T(8,128)}) custom-call(f32[2048,768]{1,0:T(8,128)} %get-tuple-element.49.gated_ref, f32[2048,768]{1,0:T(8,128)} %cotangent_ref.5, f32[8,2048]{1,0:T(8,128)} %get-tuple-element.50.own_ref, f32[8,2048]{1,0:T(8,128)} %copy-done.3, f32[1,768]{1,0:T(1,128)} %reshape.57.gated_norm_ref), custom_call_target="tpu_custom_call" | custom-call | tf_op jit(solution)/shard_map/grad_out_weight/pallas_call | solution.py:320
  70.5 21.7 %grad_gate.1 = (f32[2048,768]{1,0:T(8,128)}, bf16[2048,768]{1,0:T(8,128)(2,1)}, f32[2048,768]{1,0:T(8,128)}, f32[768,768]{1,0:T(8,128)}, f32[1,768]{1,0:T(1,128)}) custom-call(bf16[2048,768]{1,0:T(8,128)(2,1)} %get-tuple-element.46.normed_ref, bf16[2048,768]{1,0:T(8,128)(2,1)} %get-tuple-element.51.scaled_ref, f32[2048,768]{1,0:T(8,128)} %get-tuple-element.49.gated_ref, ...), custom_call_target="tpu_custom_call" | custom-call | tf_op jit(solution)/shard_map/grad_gate/pallas_call | solution.py:379
  92.3 59.7 %scan_back.1 = (bf16[2048,768]{1,0:T(8,128)(2,1)}, bf16[2048,128]{1,0:T(8,128)(2,1)}, f32[2048,256]{1,0:T(8,128)}, f32[3,768,256]{2,1,0:T(8,128)}, f32[768,128]{...) custom-call(bf16[2048,768]{1,0:T(8,128)(2,1)} %get-tuple-element.46.normed_ref, ...), custom_call_target="tpu_custom_call" | custom-call | tf_op jit(solution)/shard_map/scan_back/pallas_call | solution.py:568
  152.0 1.7 slice_select_fusion
  153.9 2.5 collective-permute-done.1.other_ref
  156.4 1.0 copy-done.2
  157.4 15.2 %grad_in.1 = (f32[2048,768]{1,0:T(8,128)}, f32[768,128]{1,0:T(8,128)}, f32[8,128]{1,0:T(8,128)}) custom-call(s32[1]{0:T(128)} %bitcast.core_ref, f32[2048,256]{1,0:T(8,128)} %get-tuple-element.58.own_ref, f32[2048,128]{1,0:T(8,128)} %copy-done.2, f32[2048,256]{1,0:T(8,128)} %get-tuple-element.47.state_raw_ref, ...), custom_call_target="tpu_custom_call" | custom-call | tf_op jit(solution)/shard_map/grad_in/pallas_call | solution.py:660
  173.2 9.9 %collective-permute-done.3.out_other_ref = f32[2048,768]{1,0:T(8,128)} collective-permute-done((f32[2048,768]{1,0:T(8,128)}, f32[2048,768]{1,0:T(8,128)}, u32[]{:S(2)}, u32[]{:S(2)}) %collective-permute-start.3) | collective-permute-done | bytes 6291488 | tf_op jit(solution)/shard_map/ppermute | solution.py:741
  183.1 9.0 %collective-permute-done.2.other_ref = f32[2048,768]{1,0:T(8,128)} collective-permute-done((f32[2048,768]{1,0:T(8,128)}, f32[2048,768]{1,0:T(8,128)}, u32[]{:S(2)}, u32[]{:S(2)}) %collective-permute-start.2) | collective-permute-done | bytes 6291488 | tf_op jit(solution)/shard_map/ppermute | solution.py:741
  192.1 18.3 %grad_hidden.1 = (f32[2048,768]{1,0:T(8,128)}, f32[2048,768]{1,0:T(8,128)}, f32[1,768]{1,0:T(1,128)}) custom-call(f32[2048,768]{1,0:T(8,128)} %hidden_ref.3, f32[2048,768]{1,0:T(8,128)} %cotangent_ref.5, f32[2048,768]{1,0:T(8,128)} %get-tuple-element.62.own_ref, f32[2048,768]{1,0:T(8,128)} %collective-permute-done.2.other_ref, ...), custom_call_target="tpu_custom_call" | custom-call | tf_op jit(solution)/shard_map/grad_hidden/pallas_call | solution.py:722
  210.4 0.7 reduce
  211.1 68.5 %all-reduce.2 = (f32[768]{0:T(1024)}, f32[8,128]{1,0:T(8,128)S(1)}, f32[3,8,256]{2,1,0:T(8,128)S(1)}, f32[8,128]{1,0:T(8,128)S(1)}, f32[768]{0:T(1024)}) all-reduce(f32[768]{0:T(1024)S(1)} %reduce, f32[8,128]{1,0:T(8,128)S(1)} %copy-done.6, f32[3,8,256]{2,1,0:T(8,128)S(1)} %copy-done.4, ...), channel_id=1, replica_groups=mesh['dp'=16,'tensor'=2] {'dp'}, use_global_device_ids=true, to_apply=%region_0.1 | all-reduce | flops 9728 | bytes 77824 | tf_op jit(solution)/shard_map/psum | solution.py:786
  282.1 141.7 %all-reduce.6.cloned.1.call-done = (f32[768,768]{1,0:T(8,128)}, f32[3,768,256]{2,1,0:T(8,128)}, f32[768,128]{1,0:T(8,128)}, f32[768,128]{1,0:T(8,128)}, f32[768,768]{1,0:T(8,128)}) async-done(((f32[768,768]{1,0:T(8,128)}, f32[3,768,256]{2,1,0:T(8,128)}, f32[768,128]{1,0:T(8,128)}, f32[768,128]{1,0:T(8,128)}, f32[768,768]{1,0:T(8,128)}), (f32[768,768]{1,0:T(8,128)}, f32[3,768,256]{2,1,0:T(8,128)}, ...) | async-done | bytes 7864336 | tf_op jit(solution)/shard_map/psum | solution.py:786
  423.8 1.0 constant_dynamic-update-slice_fusion.1
  424.8 0.7 collective-permute-start.4
  425.6 1.8 copy.33
  427.3 1.8 slice_bitcast_fusion.2
  429.1 1.6 pad_maximum_fusion
  430.8 0.9 slice.71
  432.8 1.4 copy.40
  434.3 1.1 copy-done
  435.4 1.4 copy.41
  (34 shorter events, 6.1 us)
Async XLA Ops:
  7.2 416.6 %all-reduce.6.cloned.1.call-start = ((), (), s32[]{:S(2)}) async-start(), calls=%async_computation | async-start | bytes 15728640 | tf_op jit(solution)/shard_map/psum | solution.py:786
  57.7 1.5 collective-permute-start
  59.3 0.6 copy-start.3
  153.7 2.7 collective-permute-start.1
  156.4 1.0 copy-start.2
  172.5 0.7 copy-start.7
  172.5 10.6 %collective-permute-start.3 = (f32[2048,768]{1,0:T(8,128)}, f32[2048,768]{1,0:T(8,128)}, u32[]{:S(2)}, u32[]{:S(2)}) collective-permute-start(f32[2048,768]{1,0:T(8,128)} %get-tuple-element.63.out_own_ref), channel_id=1, source_target_pairs={{0,1},{1,0},{2,3},{3,2},{4,5},{5,4},{6,7},{7,6},{8,9},{9,8},{10,11... | collective-permute-start | bytes 18874376 | tf_op jit(solution)/shard_map/ppermute | solution.py:741
  172.8 19.3 %collective-permute-start.2 = (f32[2048,768]{1,0:T(8,128)}, f32[2048,768]{1,0:T(8,128)}, u32[]{:S(2)}, u32[]{:S(2)}) collective-permute-start(f32[2048,768]{1,0:T(8,128)} %get-tuple-element.62.own_ref), channel_id=1, source_target_pairs={{0,1},{1,0},{2,3},{3,2},{4,5},{5,4},{6,7},{7,6},{8,9},{9,8},{10,11... | collective-permute-start | bytes 18874376 | tf_op jit(solution)/shard_map/ppermute | solution.py:741
  173.2 37.9 %copy-start.4 = (f32[3,8,256]{2,1,0:T(8,128)S(1)}, f32[3,8,256]{2,1,0:T(8,128)}, u32[]{:S(2)}) copy-start(f32[3,8,256]{2,1,0:T(8,128)} %get-tuple-element.72) | copy-start | bytes 73732
  173.2 37.9 %copy-start.5 = (f32[8,128]{1,0:T(8,128)S(1)}, f32[8,128]{1,0:T(8,128)}, u32[]{:S(2)}) copy-start(f32[8,128]{1,0:T(8,128)} %get-tuple-element.73) | copy-start | bytes 12292
  173.2 37.9 %copy-start.6 = (f32[8,128]{1,0:T(8,128)S(1)}, f32[8,128]{1,0:T(8,128)}, u32[]{:S(2)}) copy-start(f32[8,128]{1,0:T(8,128)} %get-tuple-element.70) | copy-start | bytes 12292
  424.8 5.8 %collective-permute-start.4 = (f32[776,128]{1,0:T(8,128)S(1)}, f32[776,128]{1,0:T(8,128)S(1)}, u32[]{:S(2)}, u32[]{:S(2)}) collective-permute-start(f32[776,128]{1,0:T(8,128)S(1)} %constant_dynamic-update-slice_fusion), channel_id=1, source_target_pairs={{0,1},{1,0},{2,3},{3,2},{4,5},{5,4},{6,7},{7,6},{8,9},{9,8},{10,11... | collective-permute-start | bytes 1191944 | tf_op jit(solution)/shard_map/ppermute | solution.py:741
  430.6 2.2 copy-start.1
  432.8 2.5 copy-start
Sparse Core Ops, SparseCore 0:
  172.7 251.0 all-reduce.5

commit v2 on v1

v2 whole, which is shorter than its diff:
```python
import functools

import jax
import jax.numpy as jnp
from jax import lax
from jax.experimental import pallas as pl
from jax.experimental.pallas import tpu as pltpu
from jax.sharding import PartitionSpec as P

HEAD_DIM = 64
STATE = 128
LENGTH = 512
STRIP = 128
WIDTH = 256
GROUP_HEADS = WIDTH // HEAD_DIM
EPSILON = 1e-05
F32 = jnp.float32
BF16 = jnp.bfloat16
MIB = 1 << 20
TAPS = 4
NORM, OFFSET, GAIN, SKIP, KERNEL = range(5)


def dot_nn(left, right):
    return lax.dot_general(left, right, (((1,), (0,)), ((), ())), preferred_element_type=F32)


def dot_nt(left, right):
    return lax.dot_general(left, right, (((1,), (1,)), ((), ())), preferred_element_type=F32)


def dot_tn(left, right):
    return lax.dot_general(left, right, (((0,), (0,)), ((), ())), preferred_element_type=F32)


def split2(value):
    high = value.astype(BF16)
    return high, (value - high.astype(F32)).astype(BF16)


def split3(value):
    high = value.astype(BF16)
    rest = value - high.astype(F32)
    middle = rest.astype(BF16)
    return high, middle, (rest - middle.astype(F32)).astype(BF16)


def dot3(dot, left, right):
    left_high, left_low = split2(left)
    right_high, right_low = split2(right)
    return dot(left_high, right_high) + (dot(left_high, right_low) + dot(left_low, right_high))


def sigmoid(value):
    return 1.0 / (1.0 + jnp.exp(-value))


def softplus(value):
    return jnp.maximum(value, 0.0) + jnp.log1p(jnp.exp(-jnp.abs(value)))


def triangular(rows, keep_lower):
    down = lax.broadcasted_iota(jnp.int32, (rows, rows), 0)
    along = lax.broadcasted_iota(jnp.int32, (rows, rows), 1)
    return down >= along if keep_lower else down <= along


def running_sum(value, keep_lower):
    high, middle, low = split3(value)
    packed = (
        high.astype(F32)
        + pltpu.roll(middle.astype(F32), 16, 1)
        + pltpu.roll(low.astype(F32), 32, 1)
    ).astype(BF16)
    ones = jnp.where(triangular(value.shape[0], keep_lower), 1.0, 0.0).astype(BF16)
    sums = dot_nn(ones, packed)
    total = sums + pltpu.roll(sums, 128 - 16, 1) + pltpu.roll(sums, 128 - 32, 1)
    lanes = lax.broadcasted_iota(jnp.int32, total.shape, 1)
    return jnp.where(lanes < 16, total, 0.0)


def spread(columns):
    rows = columns.shape[0]
    lanes = lax.broadcasted_iota(jnp.int32, (rows, 128), 1)
    halves = []
    for pair in range(GROUP_HEADS // 2):
        first = jnp.broadcast_to(columns[:, 2 * pair : 2 * pair + 1], (rows, 128))
        second = jnp.broadcast_to(columns[:, 2 * pair + 1 : 2 * pair + 2], (rows, 128))
        halves.append(jnp.where(lanes < HEAD_DIM, first, second))
    return jnp.concatenate(halves, axis=1)


def head_only(value, head):
    lanes = lax.broadcasted_iota(jnp.int32, value.shape, 1)
    return jnp.where((lanes >= head * HEAD_DIM) & (lanes < (head + 1) * HEAD_DIM), value, 0.0).astype(BF16)


def shifted_down(value, by):
    if by == 0:
        return value
    rows = lax.broadcasted_iota(jnp.int32, value.shape, 0)
    return jnp.where(rows >= by, pltpu.roll(value, by, 0), 0.0)


def shifted_up(value, by):
    if by == 0:
        return value
    count = value.shape[0]
    rows = lax.broadcasted_iota(jnp.int32, value.shape, 0)
    return jnp.where(rows < count - by, pltpu.roll(value, count - by, 0), 0.0)


def convolve(value, kernel, offset):
    taps = kernel.shape[0]
    total = offset + kernel[taps - 1 : taps] * value
    for tap in range(taps - 1):
        total = total + kernel[tap : tap + 1] * shifted_down(value, taps - 1 - tap)
    return total


def convolve_back(grad_out, value, kernel):
    taps = kernel.shape[0]
    grad_in = kernel[taps - 1 : taps] * grad_out
    rows = []
    for tap in range(taps):
        by = taps - 1 - tap
        if by:
            grad_in = grad_in + kernel[tap : tap + 1] * shifted_up(grad_out, by)
        rows.append(jnp.sum(grad_out * shifted_down(value, by), axis=0, keepdims=True))
    rows.append(jnp.sum(grad_out, axis=0, keepdims=True))
    rows.append(jnp.zeros((8 - taps - 1, grad_out.shape[1]), F32))
    return grad_in, jnp.concatenate(rows, axis=0)


def forward_kernel(
    hidden_ref, cotangent_ref, norm_ref, vectors_ref, state_vectors_ref, heads_ref, gate_in_ref, value_in_ref,
    state_in_ref, step_in_ref, out_weight_ref,
    normed_ref, state_raw_ref, conv_ref, pair_t_ref, value_raw_ref, gate_raw_ref, mixed_ref, gated_ref,
    grad_scaled_ref, step_pre_ref, steps_ref, log_ref, sums_ref,
    upstream_s, pair_s, steps_s, log_s, log_t_s, squares_s, terms_s,
):
    group = pl.program_id(1)

    @pl.when(group == 0)
    def _():
        rows = hidden_ref[...]
        scale = lax.rsqrt(jnp.mean(rows * rows, axis=-1, keepdims=True) + EPSILON)
        normed = (rows * scale * norm_ref[NORM : NORM + 1, :]).astype(BF16)
        normed_ref[...] = normed
        upstream_s[...] = cotangent_ref[...].astype(BF16)
        raw = dot_nn(normed, state_in_ref[...])
        state_raw_ref[...] = raw
        pre = convolve(raw, state_vectors_ref[:TAPS, :], state_vectors_ref[TAPS : TAPS + 1, :])
        conv = pre * sigmoid(pre)
        conv_ref[...] = conv
        pair = dot3(dot_nt, conv[:, STATE:], conv[:, :STATE])
        pair_s[...] = jnp.where(triangular(LENGTH, True), pair, 0.0)
        pair = dot3(dot_nt, conv[:, :STATE], conv[:, STATE:])
        pair_t_ref[...] = jnp.where(triangular(LENGTH, False), pair, 0.0)
        step_pre = dot_nt(normed, step_in_ref[...]) + heads_ref[0:1, :]
        step_pre_ref[...] = step_pre
        lanes = lax.broadcasted_iota(jnp.int32, step_pre.shape, 1)
        steps = jnp.where(lanes < 12, softplus(step_pre), 0.0)
        steps_ref[...] = steps
        log = running_sum(steps * heads_ref[1:2, :], True)
        log_ref[...] = log
        transposed = log.T
        for g in range(steps_s.shape[0]):
            back = (128 - GROUP_HEADS * g) % 128
            steps_s[g] = pltpu.roll(steps, back, 1) if back else steps
            log_s[g] = pltpu.roll(log, back, 1) if back else log
            log_t_s[g] = transposed[GROUP_HEADS * g : GROUP_HEADS * g + 8]
        squares_s[...] = jnp.zeros_like(squares_s)
        terms_s[...] = jnp.zeros_like(terms_s)

    normed = normed_ref[...]
    raw = dot_nn(normed, value_in_ref[...])
    value_raw_ref[...] = raw
    pre = convolve(raw, vectors_ref[KERNEL : KERNEL + TAPS, :], vectors_ref[OFFSET : OFFSET + 1, :])
    values = pre * sigmoid(pre)
    weighted = values * spread(steps_s[group])
    parts = [head_only(weighted, head) for head in range(GROUP_HEADS)]
    log = log_s[group]
    log_t = log_t_s[group]
    strips = []
    for strip in range(LENGTH // STRIP):
        low, high = strip * STRIP, (strip + 1) * STRIP
        pair = pair_s[low:high, :high]
        weights = []
        for head in range(GROUP_HEADS):
            gap = jnp.minimum(log[low:high, head : head + 1] - log_t[head : head + 1, :high], 0.0)
            weights.append((jnp.exp(gap) * pair).astype(BF16))
        strips.append(
            dot_nn(
                jnp.concatenate(weights, axis=1),
                jnp.concatenate([part[:high] for part in parts], axis=0),
            )
        )
    mixed = jnp.concatenate(strips, axis=0) + vectors_ref[SKIP : SKIP + 1, :] * values
    mixed_ref[...] = mixed
    gate = dot_nn(normed, gate_in_ref[...])
    gate_raw_ref[...] = gate
    gated = mixed * (gate * sigmoid(gate))
    gated_ref[...] = gated
    grad_scaled = dot_nt(upstream_s[...], out_weight_ref[...])
    grad_scaled_ref[...] = grad_scaled
    squares = gated * gated
    terms = grad_scaled * vectors_ref[GAIN : GAIN + 1, :] * gated
    squares_s[...] += squares[:, :128] + squares[:, 128:]
    terms_s[...] += terms[:, :128] + terms[:, 128:]

    @pl.when(group == pl.num_programs(1) - 1)
    def _():
        lanes = lax.broadcasted_iota(jnp.int32, (LENGTH, 128), 1)
        both = jnp.where(
            lanes == 0,
            jnp.sum(squares_s[...], axis=1, keepdims=True),
            jnp.where(lanes == 1, jnp.sum(terms_s[...], axis=1, keepdims=True), 0.0),
        )
        sums_ref[...] = both.T[:8]


def cost(micros):
    return pl.CostEstimate(
        flops=int(micros * 3.0e9), transcendentals=0, bytes_accessed=int(micros * 9.0e6)
    )


def const_spec(shape):
    return pl.BlockSpec(shape, lambda *_: (0,) * len(shape))


def shape_of(*dims, dtype=F32):
    return jax.ShapeDtypeStruct(dims, dtype)


def bit_orders(count):
    bits = count.bit_length() - 1
    return list(range(bits)), list(range(1, bits)) + [0]


def cut_shapes(rows, columns):
    return [shape_of(rows // 2, columns)] * 2


def cut_into(source, bits, outs):
    half = source.shape[0] // 2
    outs[0][...] = source[pl.ds(pl.multiple_of((1 - bits[0]) * half, 8), half), :]
    outs[1][...] = source[pl.ds(pl.multiple_of(bits[0] * half, 8), half), :]


def sum_kernel(step, bits, keep_ref, came_ref, send_ref, next_ref):
    half = keep_ref.shape[0] // 2
    other = pl.ds(pl.multiple_of((1 - bits[step]) * half, 8), half)
    mine = pl.ds(pl.multiple_of(bits[step] * half, 8), half)
    send_ref[...] = keep_ref[other, :] + came_ref[other, :]
    next_ref[...] = keep_ref[mine, :] + came_ref[mine, :]


def join_last(bits, own, came, out, start, rows, offset=0):
    out[pl.ds(pl.multiple_of(start + bits[0] * rows, 8), rows), :] = own[offset : offset + rows, :]
    out[pl.ds(pl.multiple_of(start + (1 - bits[0]) * rows, 8), rows), :] = came[offset : offset + rows, :]


def total_kernel(bits, keep_ref, came_ref, out_ref):
    out_ref[...] = keep_ref[...] + came_ref[...]


def join_kernel(step, bits, own_ref, came_ref, out_ref):
    half = own_ref.shape[0]
    out_ref[pl.ds(pl.multiple_of(bits[step] * half, 8), half), :] = own_ref[...]
    out_ref[pl.ds(pl.multiple_of((1 - bits[step]) * half, 8), half), :] = came_ref[...]


def small_call(kernel, scalars, arrays, out_shape, name):
    return pl.pallas_call(
        kernel,
        grid_spec=pltpu.PrefetchScalarGridSpec(
            num_scalar_prefetch=1,
            grid=(1,),
            in_specs=[const_spec(a.shape) for a in arrays],
            out_specs=[const_spec(s.shape) for s in out_shape],
        ),
        out_shape=out_shape,
        compiler_params=pltpu.CompilerParams(vmem_limit_bytes=40 * MIB),
        cost_estimate=cost(0.1),
        name=name,
    )(scalars, *arrays)


def tie(value, *after):
    return lax.optimization_barrier((value, *after))[0]


class Reduction:
    def __init__(self, pieces, bits, count, name):
        self.sent, self.held = pieces
        self.bits, self.count, self.name = bits, count, name
        self.orders = bit_orders(count)
        self.steps = len(self.orders[0])
        self.step = 0
        self.send(0)

    def send(self, step):
        pairs = [
            (2 * i + core, 2 * (i ^ (1 << self.orders[core][step])) + core)
            for i in range(self.count) for core in range(2)
        ]
        self.came = lax.ppermute(self.sent, ("dp", "tensor"), pairs)

    def advance(self, *after):
        if self.step == 2 * self.steps - 1:
            return self.held
        self.step += 1
        steps, step = self.steps, self.step
        held = tie(self.held, *after) if after else self.held
        rows, columns = held.shape
        if step < steps:
            self.sent, self.held = small_call(
                functools.partial(sum_kernel, step), self.bits, [held, self.came],
                [shape_of(rows // 2, columns)] * 2, self.name + "_sum",
            )
            self.send(step)
        elif step == steps:
            (self.held,) = small_call(
                total_kernel, self.bits, [held, self.came], [shape_of(rows, columns)], self.name + "_total"
            )
            self.sent = self.held
            self.send(steps - 1)
        else:
            back = 2 * steps - step
            (self.held,) = small_call(
                functools.partial(join_kernel, back), self.bits, [held, self.came],
                [shape_of(2 * rows, columns)], self.name + "_join",
            )
            self.sent = self.held
            self.send(back - 1)
        return self.held

    def halves(self):
        while self.step < 2 * self.steps - 1:
            self.advance()
        return self.held, self.came


class PlainReduction:
    def __init__(self, pieces, bits, count, name):
        self.sent, self.held = lax.psum(tuple(pieces), "dp")

    def advance(self, *after):
        return self.held

    def halves(self):
        return self.held, self.sent


def run_forward(hidden, cotangent, vectors, state_vectors, heads, gate_in, value_in, state_in, step_in, out_weight):
    tokens, width = hidden.shape
    channels = gate_in.shape[1]
    groups = channels // WIDTH
    sequences = tokens // LENGTH
    row = lambda s, g: (s, 0)
    block = lambda s, g: (s, g)
    column = lambda s, g: (0, g)
    wide = shape_of(tokens, channels)
    narrow = shape_of(tokens, 128)
    wide_spec = pl.BlockSpec((LENGTH, WIDTH), block)
    narrow_spec = pl.BlockSpec((LENGTH, 128), row)
    return pl.pallas_call(
        forward_kernel,
        grid=(sequences, groups),
        in_specs=[
            pl.BlockSpec((LENGTH, width), row),
            pl.BlockSpec((LENGTH, width), row),
            const_spec((8, width)),
            pl.BlockSpec((8, WIDTH), column),
            const_spec((8, 2 * STATE)),
            const_spec((8, 128)),
            pl.BlockSpec((width, WIDTH), column),
            pl.BlockSpec((width, WIDTH), column),
            const_spec((width, 2 * STATE)),
            const_spec((128, width)),
            pl.BlockSpec((WIDTH, width), lambda s, g: (g, 0)),
        ],
        out_specs=[
            pl.BlockSpec((LENGTH, width), row),
            pl.BlockSpec((LENGTH, 2 * STATE), row),
            pl.BlockSpec((LENGTH, 2 * STATE), row),
            pl.BlockSpec((LENGTH, LENGTH), row),
            wide_spec,
            wide_spec,
            wide_spec,
            wide_spec,
            wide_spec,
            narrow_spec,
            narrow_spec,
            narrow_spec,
            pl.BlockSpec((8, LENGTH), lambda s, g: (0, s)),
        ],
        out_shape=[
            shape_of(tokens, width, dtype=BF16),
            shape_of(tokens, 2 * STATE),
            shape_of(tokens, 2 * STATE),
            shape_of(tokens, LENGTH),
            wide,
            wide,
            wide,
            wide,
            wide,
            narrow,
            narrow,
            narrow,
            shape_of(8, tokens),
        ],
        scratch_shapes=[
            pltpu.VMEM((LENGTH, width), BF16),
            pltpu.VMEM((LENGTH, LENGTH), F32),
            pltpu.VMEM((groups, LENGTH, 128), F32),
            pltpu.VMEM((groups, LENGTH, 128), F32),
            pltpu.VMEM((groups, 8, LENGTH), F32),
            pltpu.VMEM((LENGTH, 128), F32),
            pltpu.VMEM((LENGTH, 128), F32),
        ],
        compiler_params=pltpu.CompilerParams(vmem_limit_bytes=56 * MIB),
        cost_estimate=cost(45),
        name="forward_mix",
    )(hidden, cotangent, vectors, vectors, state_vectors, heads, gate_in, value_in, state_in, step_in, out_weight)


def row_factors(own_ref, other_ref, inner):
    sums = own_ref[...] + other_ref[...]
    columns = jnp.concatenate([sums, jnp.zeros((120, sums.shape[1]), F32)], axis=0).T
    scale = lax.rsqrt(columns[:, 0:1] / inner + EPSILON)
    return scale, columns[:, 1:2] * (scale * scale * scale) / inner


def along_rows(column):
    return jnp.broadcast_to(column, (column.shape[0], 128)).T[:8]


def norm_back_kernel(
    inner, digits, normed_ref, gated_ref, mixed_ref, gate_ref, grad_scaled_ref, cotangent_ref, own_ref, other_ref,
    vectors_ref, gate_in_ref, out_weight_ref,
    grad_mixed_ref, gate_low_ref, partial_ref, grad_norm_ref, norm_rows_ref, send_ref, keep_ref, out_s, gate_s,
):
    @pl.when(pl.program_id(0) == 0)
    def _():
        out_s[...] = jnp.zeros_like(out_s)
        gate_s[...] = jnp.zeros_like(gate_s)
        grad_norm_ref[...] = jnp.zeros_like(grad_norm_ref)

    scale, factor = row_factors(own_ref, other_ref, inner)
    normed_t = normed_ref[...].T
    upstream = cotangent_ref[...].astype(BF16)
    partial = None
    for group in range(gated_ref.shape[1] // WIDTH):
        columns = slice(group * WIDTH, (group + 1) * WIDTH)
        gated = gated_ref[:, columns]
        gate = gate_ref[:, columns]
        gain = vectors_ref[GAIN : GAIN + 1, columns]
        scaled = (gated * scale * gain).astype(BF16)
        out_s[columns, :] += dot_tn(scaled, upstream)
        product = dot_nn(scaled, out_weight_ref[columns, :])
        partial = product if partial is None else partial + product
        scaled_by = grad_scaled_ref[:, columns] * scale
        grad_norm_ref[:, columns] += jnp.broadcast_to(
            jnp.sum(scaled_by * gated, axis=0, keepdims=True), (8, WIDTH)
        )
        grad_gated = scaled_by * gain - gated * factor
        s = sigmoid(gate)
        grad_mixed_ref[:, columns] = grad_gated * (gate * s)
        low = (grad_gated * mixed_ref[:, columns] * (s * (1.0 + gate * (1.0 - s)))).astype(BF16)
        gate_low_ref[:, columns] = low
        gate_s[:, columns] += dot_nn(normed_t, low)
    partial_ref[...] = partial

    @pl.when(pl.program_id(0) == pl.num_programs(0) - 1)
    def _():
        half = gate_s.shape[0] // 2
        other = pl.ds(pl.multiple_of((1 - digits[0]) * half, 8), half)
        mine = pl.ds(pl.multiple_of(digits[0] * half, 8), half)
        for k, source in enumerate((out_s, gate_s)):
            send_ref[k * half : (k + 1) * half, :] = source[other, :]
            keep_ref[k * half : (k + 1) * half, :] = source[mine, :]
        norm_rows_ref[...] = along_rows(
            jnp.sum(gate_s[...] * gate_in_ref[...].astype(F32), axis=1, keepdims=True)
        )


def run_norm_back(digits, normed, gated, mixed, gate_raw, grad_scaled, cotangent, own, other, vectors, gate_in,
                  out_weight, inner):
    tokens, channels = gated.shape
    width = normed.shape[1]
    row = lambda s, _: (s, 0)
    wide = pl.BlockSpec((LENGTH, channels), row)
    rows = (width + channels) // 2
    return pl.pallas_call(
        functools.partial(norm_back_kernel, inner),
        grid_spec=pltpu.PrefetchScalarGridSpec(
            num_scalar_prefetch=1,
            grid=(tokens // LENGTH,),
            in_specs=[
                pl.BlockSpec((LENGTH, width), row),
                wide,
                wide,
                wide,
                wide,
                pl.BlockSpec((LENGTH, width), row),
                pl.BlockSpec((8, LENGTH), lambda s, _: (0, s)),
                pl.BlockSpec((8, LENGTH), lambda s, _: (0, s)),
                const_spec((8, channels)),
                const_spec((width, channels)),
                const_spec((channels, width)),
            ],
            out_specs=[
                wide,
                wide,
                pl.BlockSpec((LENGTH, width), row),
                const_spec((8, channels)),
                const_spec((8, width)),
                const_spec((rows, width)),
                const_spec((rows, width)),
            ],
            scratch_shapes=[pltpu.VMEM((channels, width), F32), pltpu.VMEM((width, channels), F32)],
        ),
        out_shape=[
            shape_of(tokens, channels),
            shape_of(tokens, channels, dtype=BF16),
            shape_of(tokens, width),
            shape_of(8, channels),
            shape_of(8, width),
            shape_of(rows, width),
            shape_of(rows, width),
        ],
        compiler_params=pltpu.CompilerParams(vmem_limit_bytes=60 * MIB),
        cost_estimate=cost(26),
        name="norm_back",
    )(digits, normed, gated, mixed, gate_raw, grad_scaled, cotangent, own, other, vectors, gate_in, out_weight)


def scan_back_kernel(
    group, groups, digits, normed_ref, pair_ref, value_raw_ref, grad_mixed_ref, steps_ref, log_ref, vectors_ref,
    value_in_ref, *refs,
):
    first, last = group == 0, group == groups - 1
    refs = list(refs)
    take = lambda count: [refs.pop(0) for _ in range(count)]
    if not first:
        _, grad_pair_before = take(2)
    if group == 1:
        (value_before,) = take(1)
    if last:
        conv_ref, step_pre_ref, heads_ref, step_in_ref = take(4)
        rows_before, columns_before, direct_before = take(group), take(group), take(group)
    (value_low_ref,) = take(1)
    if not last:
        grad_pair_ref, row_sums_ref, column_sums_ref, direct_ref = take(4)
    value_outs = take(2 if group == 1 else 1)
    rows_ref, norm_rows_ref = take(2)
    if last:
        step_low_ref, mine_ref, other_ref, grad_step_ref, head_rows_ref = take(5)
    grad_value_s, grad_pair_s = take(2)
    sequence = pl.program_id(0)

    @pl.when(sequence == 0)
    def _():
        grad_value_s[...] = jnp.zeros_like(grad_value_s)
        rows_ref[...] = jnp.zeros_like(rows_ref)
        if last:
            grad_step_ref[...] = jnp.zeros_like(grad_step_ref)
            head_rows_ref[...] = jnp.zeros_like(head_rows_ref)

    place = group * GROUP_HEADS
    back = (128 - place) % 128
    group_steps, log = steps_ref[...], log_ref[...]
    log_t = log.T[place : place + GROUP_HEADS]
    if back:
        group_steps, log = pltpu.roll(group_steps, back, 1), pltpu.roll(log, back, 1)
    raw = value_raw_ref[...]
    kernel = vectors_ref[KERNEL : KERNEL + TAPS, :]
    pre = convolve(raw, kernel, vectors_ref[OFFSET : OFFSET + 1, :])
    s = sigmoid(pre)
    values = pre * s
    steps = spread(group_steps)
    weighted = values * steps
    grad_mixed = grad_mixed_ref[...]
    grad_low = grad_mixed.astype(BF16)
    weighted_parts = [head_only(weighted, head) for head in range(GROUP_HEADS)]
    grad_parts = [head_only(grad_mixed, head) for head in range(GROUP_HEADS)]
    strips = []
    columns = []
    row_sums = [jnp.zeros((1, LENGTH), F32) for _ in range(GROUP_HEADS)]
    for strip in range(LENGTH // STRIP):
        low, high = strip * STRIP, (strip + 1) * STRIP
        pair = pair_ref[low:high, low:]
        total = None
        products = []
        sums = []
        for head in range(GROUP_HEADS):
            gap = jnp.minimum(log_t[head : head + 1, low:] - log[low:high, head : head + 1], 0.0)
            decay = jnp.exp(gap)
            weight = decay * pair
            products.append(weight.astype(BF16))
            grad_weight = dot_nt(weighted_parts[head][low:high], grad_low[low:])
            grad_pair = grad_weight * decay
            total = grad_pair if total is None else total + grad_pair
            both = grad_weight * weight
            sums.append(jnp.sum(both, axis=1, keepdims=True))
            along = jnp.sum(both, axis=0, keepdims=True)
            if low:
                along = jnp.concatenate([jnp.zeros((1, low), F32), along], axis=1)
            row_sums[head] = row_sums[head] + along
        if not first:
            total = total + grad_pair_before[low:high, low:]
        if last:
            grad_pair_s[low:high, low:] = total
        else:
            grad_pair_ref[low:high, low:] = total
        columns.append(sums)
        strips.append(
            dot_nn(
                jnp.concatenate(products, axis=1),
                jnp.concatenate([part[low:] for part in grad_parts], axis=0),
            )
        )
    reached = jnp.concatenate(strips, axis=0)
    lanes = lax.broadcasted_iota(jnp.int32, (LENGTH, 128), 1)
    column_sums = jnp.zeros((LENGTH, 128), F32)
    for head in range(GROUP_HEADS):
        one = jnp.concatenate([sums[head] for sums in columns], axis=0)
        column_sums = jnp.where(lanes == place + head, one, column_sums)
    down = lax.broadcasted_iota(jnp.int32, (WIDTH, 128), 0)
    across = lax.broadcasted_iota(jnp.int32, (WIDTH, 128), 1)
    start = (across - place) * HEAD_DIM
    picks = jnp.where((down >= start) & (down < start + HEAD_DIM), 1.0, 0.0).astype(BF16)
    direct_high, direct_low = split2(values * reached)
    direct = dot_nn(direct_high, picks) + dot_nn(direct_low, picks)

    grad_values = steps * reached + vectors_ref[SKIP : SKIP + 1, :] * grad_mixed
    grad_pre = grad_values * (s * (1.0 + pre * (1.0 - s)))
    grad_raw, rows = convolve_back(grad_pre, raw, kernel)
    skip_rows = jnp.sum(grad_mixed * values, axis=0, keepdims=True)
    rows_ref[...] += jnp.concatenate([rows[: TAPS + 1], skip_rows, rows[TAPS + 2 :]], axis=0)
    value_low = grad_raw.astype(BF16)
    value_low_ref[...] = value_low
    grad_value_s[...] += dot_tn(value_low, normed_ref[...])

    if not last:
        row_sums_ref[...] = jnp.concatenate(row_sums + [jnp.zeros((8 - GROUP_HEADS, LENGTH), F32)], axis=0)
        column_sums_ref[...] = column_sums
        direct_ref[...] = direct
    else:
        conv = conv_ref[...]
        grad_pair = jnp.where(triangular(LENGTH, False), grad_pair_s[...], 0.0)
        grad_write = dot3(dot_nn, grad_pair, conv[:, STATE:])
        grad_read = dot3(dot_tn, grad_pair, conv[:, :STATE])
        core = digits[digits.shape[0] - 1]
        mine_ref[...] = jnp.where(core == 0, grad_write, grad_read)
        other_ref[...] = jnp.where(core == 0, grad_read, grad_write)
        for before in columns_before:
            column_sums = column_sums + before[...]
        for before in direct_before:
            direct = direct + before[...]
        row_sums = jnp.concatenate(
            [before[:GROUP_HEADS, :] for before in rows_before]
            + row_sums
            + [jnp.zeros((128 - GROUP_HEADS * groups, LENGTH), F32)],
            axis=0,
        ).T
        memory = running_sum(row_sums - column_sums, False)
        step_pre = step_pre_ref[...]
        rate = heads_ref[1:2, :]
        grad_raw = jnp.where(lanes < 12, (direct + rate * memory) * sigmoid(step_pre), 0.0)
        step_low = grad_raw.astype(BF16)
        step_low_ref[...] = step_low
        grad_step_ref[...] += dot_tn(step_low, normed_ref[...])[:16]
        decay_row = rate * jnp.sum(steps_ref[...] * memory, axis=0, keepdims=True)
        head_rows_ref[...] += jnp.concatenate(
            [jnp.sum(grad_raw, axis=0, keepdims=True), decay_row, jnp.zeros((6, 128), F32)], axis=0
        )

    @pl.when(sequence == pl.num_programs(0) - 1)
    def _():
        grad_value = grad_value_s[...].T
        norm_column = jnp.sum(grad_value * value_in_ref[...].astype(F32), axis=1, keepdims=True)
        norm_rows = along_rows(norm_column)
        if last:
            product = grad_step_ref[...] * step_in_ref[:16, :].astype(F32)
            norm_rows = norm_rows + jnp.broadcast_to(jnp.sum(product, axis=0, keepdims=True), norm_rows.shape)
        norm_rows_ref[...] = norm_rows
        if group == 1:
            send_ref, keep_ref = value_outs
            half = send_ref.shape[0]
            other = pl.ds(pl.multiple_of((1 - digits[0]) * half, 8), half)
            mine = pl.ds(pl.multiple_of(digits[0] * half, 8), half)
            send_ref[:, :WIDTH] = value_before[other, :]
            keep_ref[:, :WIDTH] = value_before[mine, :]
            low, high = grad_value[:half], grad_value[half:]
            send_ref[:, WIDTH:] = jnp.where(digits[0] == 0, high, low)
            keep_ref[:, WIDTH:] = jnp.where(digits[0] == 0, low, high)
        else:
            value_outs[0][...] = grad_value


def run_scan_back(group, groups, digits, normed, pair, value_raw, grad_mixed, steps, log, vectors, value_in,
                  value_low, grad_pair, first_value, extra):
    tokens, width = normed.shape
    channels = value_raw.shape[1]
    first, last = group == 0, group == groups - 1
    row = lambda s, _: (s, 0)
    block = lambda s, _: (s, group)
    column = lambda s, _: (0, group)
    along = lambda s, _: (0, s)
    whole_row = lambda array: pl.BlockSpec((LENGTH, array.shape[1]), row)
    narrow = pl.BlockSpec((LENGTH, 128), row)
    sums = pl.BlockSpec((8, LENGTH), along)
    arrays = [normed, pair, value_raw, grad_mixed, steps, log, vectors, value_in]
    in_specs = [
        whole_row(normed),
        whole_row(pair),
        pl.BlockSpec((LENGTH, WIDTH), block),
        pl.BlockSpec((LENGTH, WIDTH), block),
        narrow,
        narrow,
        pl.BlockSpec((8, WIDTH), column),
        pl.BlockSpec((width, WIDTH), column),
    ]
    aliases = {}
    if not first:
        aliases = {1 + len(arrays): 0}
        arrays += [value_low, grad_pair]
        in_specs += [pl.BlockSpec(memory_space=pl.ANY), whole_row(grad_pair)]
    if group == 1:
        arrays.append(first_value)
        in_specs.append(const_spec(first_value.shape))
    if last:
        conv, step_pre, heads, step_in, row_sums, column_sums, direct = extra
        arrays += [conv, step_pre, heads, step_in, *row_sums, *column_sums, *direct]
        in_specs += [whole_row(conv), narrow, const_spec(heads.shape), const_spec(step_in.shape)]
        in_specs += [sums] * group + [narrow] * (2 * group)
    shapes, specs = [shape_of(tokens, channels, dtype=BF16)], [pl.BlockSpec((LENGTH, WIDTH), block)]
    if not last:
        shapes += [shape_of(tokens, LENGTH), shape_of(8, tokens), shape_of(tokens, 128), shape_of(tokens, 128)]
        specs += [pl.BlockSpec((LENGTH, LENGTH), row), sums, narrow, narrow]
    totals = [shape_of(width // 2, 2 * WIDTH)] * 2 if group == 1 else [shape_of(width, WIDTH)]
    totals += [shape_of(8, WIDTH), shape_of(8, width)]
    shapes += totals
    specs += [const_spec(total.shape) for total in totals]
    if last:
        shapes += [shape_of(tokens, 128, dtype=BF16), shape_of(tokens, STATE), shape_of(tokens, STATE)]
        shapes += [shape_of(16, width), shape_of(8, 128)]
        specs += [narrow] * 3 + [const_spec((16, width)), const_spec((8, 128))]
    return pl.pallas_call(
        functools.partial(scan_back_kernel, group, groups),
        grid_spec=pltpu.PrefetchScalarGridSpec(
            num_scalar_prefetch=1,
            grid=(tokens // LENGTH,),
            in_specs=in_specs,
            out_specs=specs,
            scratch_shapes=[pltpu.VMEM((WIDTH, width), F32), pltpu.VMEM((LENGTH, LENGTH), F32)],
        ),
        out_shape=shapes,
        input_output_aliases=aliases,
        compiler_params=pltpu.CompilerParams(vmem_limit_bytes=60 * MIB),
        cost_estimate=cost(22),
        name="scan_back",
    )(digits, *arrays)


PACK_ROWS = 2560
SHARED_ROWS = 824


def pack_plan(width):
    chunks = width // 128
    plan, start = {}, 0
    for name, rows, parts in (
        ("state", width, 1), ("state_rows", 8, 1), ("norm", 8, chunks), ("value", width, WIDTH // 128),
        ("step", 16, chunks), ("value_rows", 8, chunks), ("gain", 8, chunks), ("heads", 8, 1),
    ):
        plan[name] = [(start + part * rows, start + (part + 1) * rows, part * 128) for part in range(parts)]
        start += rows * parts
    assert start == PACK_ROWS
    return plan


def state_kernel(
    digits, mine_ref, came_ref, raw_ref, normed_ref, state_in_ref, vectors_ref, value_ref, step_ref, gain_ref,
    heads_ref, *refs,
):
    refs = list(refs)
    value_rows, norm_rows = refs[:3], refs[3:7]
    low_ref, send_ref, keep_ref, grad_s, rows_s, packed = refs[7:]

    @pl.when(pl.program_id(0) == 0)
    def _():
        grad_s[...] = jnp.zeros_like(grad_s)
        rows_s[...] = jnp.zeros_like(rows_s)

    raw = raw_ref[...]
    kernel = vectors_ref[:TAPS, :]
    pre = convolve(raw, kernel, vectors_ref[TAPS : TAPS + 1, :])
    s = sigmoid(pre)
    grad_pre = (mine_ref[...] + came_ref[...]) * (s * (1.0 + pre * (1.0 - s)))
    grad_raw, rows = convolve_back(grad_pre, raw, kernel)
    low = grad_raw.astype(BF16)
    low_ref[...] = low
    grad_s[...] += dot_tn(low, normed_ref[...])
    rows_s[...] += rows

    @pl.when(pl.program_id(0) == pl.num_programs(0) - 1)
    def _():
        grad = grad_s[...].T
        norm = along_rows(jnp.sum(grad * state_in_ref[...].astype(F32), axis=1, keepdims=True))
        for part in norm_rows:
            norm = norm + part[...]
        sources = {
            "state": grad, "state_rows": rows_s[...], "norm": norm, "value": value_ref[...], "step": step_ref[...],
            "value_rows": jnp.concatenate([part[...] for part in value_rows], axis=1), "gain": gain_ref[...],
            "heads": heads_ref[...],
        }
        for name, parts in pack_plan(normed_ref.shape[1]).items():
            for start, stop, lane in parts:
                packed[start:stop, :] = sources[name][:, lane : lane + 128]
        cut_into(packed, digits, (send_ref, keep_ref))


def run_state(digits, core, mine, came, state_raw, normed, state_in, state_vectors, value, step, gain, heads,
              value_rows, norm_rows):
    tokens, width = normed.shape
    row = lambda s, *_: (s, 0)
    at = digits.shape[0] - 1
    half = lambda s, d: (s, d[at])
    column = lambda s, d: (0, d[at])
    consts = [value, step, gain, heads, *value_rows, *norm_rows]
    return pl.pallas_call(
        state_kernel,
        grid_spec=pltpu.PrefetchScalarGridSpec(
            num_scalar_prefetch=1,
            grid=(tokens // LENGTH,),
            in_specs=[
                pl.BlockSpec((LENGTH, STATE), row),
                pl.BlockSpec((LENGTH, STATE), row),
                pl.BlockSpec((LENGTH, STATE), half),
                pl.BlockSpec((LENGTH, width), row),
                pl.BlockSpec((width, STATE), column),
                pl.BlockSpec((8, STATE), column),
            ]
            + [const_spec(array.shape) for array in consts],
            out_specs=[pl.BlockSpec((LENGTH, STATE), row)] + [const_spec((PACK_ROWS // 2, 128))] * 2,
            scratch_shapes=[
                pltpu.VMEM((STATE, width), F32),
                pltpu.VMEM((8, STATE), F32),
                pltpu.VMEM((PACK_ROWS, 128), F32),
            ],
        ),
        out_shape=[shape_of(tokens, STATE, dtype=BF16)] + cut_shapes(PACK_ROWS, 128),
        compiler_params=pltpu.CompilerParams(vmem_limit_bytes=60 * MIB),
        cost_estimate=cost(8),
        name="state_back",
    )(digits, mine, came, state_raw, normed, state_in, state_vectors, *consts)


def in_kernel(core, gate_low_ref, value_low_ref, step_low_ref, state_low_ref, gate_in_ref, value_in_ref, step_in_ref,
              state_in_ref, partial_ref):
    partial_ref[...] = (
        dot_nt(gate_low_ref[...], gate_in_ref[...])
        + dot_nt(value_low_ref[...], value_in_ref[...])
        + dot_nn(step_low_ref[...], step_in_ref[...])
        + dot_nt(state_low_ref[...], state_in_ref[...])
    )


def run_in(part, parts, core, gate_low, value_low, step_low, state_low, gate_in, value_in, step_in, state_in):
    tokens, channels = gate_low.shape
    width = gate_in.shape[0]
    count = tokens // LENGTH // parts
    row = lambda s, c: (s + part * count, 0)
    return pl.pallas_call(
        in_kernel,
        grid_spec=pltpu.PrefetchScalarGridSpec(
            num_scalar_prefetch=1,
            grid=(count,),
            in_specs=[
                pl.BlockSpec((LENGTH, channels), row),
                pl.BlockSpec((LENGTH, channels), row),
                pl.BlockSpec((LENGTH, 128), row),
                pl.BlockSpec((LENGTH, STATE), row),
                const_spec((width, channels)),
                const_spec((width, channels)),
                const_spec((128, width)),
                pl.BlockSpec((width, STATE), lambda s, c: (0, c[0])),
            ],
            out_specs=pl.BlockSpec((LENGTH, width), lambda s, c: (s, 0)),
        ),
        out_shape=shape_of(count * LENGTH, width),
        compiler_params=pltpu.CompilerParams(vmem_limit_bytes=60 * MIB),
        cost_estimate=cost(7.5),
        name="grad_in",
    )(core, gate_low, value_low, step_low, state_low, gate_in, value_in, step_in, state_in)


def last_kernel(hidden_ref, cotangent_ref, own_ref, other_ref, out_own_ref, out_other_ref, norm_ref, *refs):
    block_ref, grad_ref = refs[-2:]
    rows = hidden_ref[...]
    block_ref[...] = rows + (out_own_ref[...] + out_other_ref[...])
    scale = lax.rsqrt(jnp.mean(rows * rows, axis=-1, keepdims=True) + EPSILON)
    product = (own_ref[...] + other_ref[...]) * norm_ref[NORM : NORM + 1, :]
    terms = jnp.sum(product * rows, axis=-1, keepdims=True)
    grad_ref[...] = (
        cotangent_ref[...] + product * scale - rows * (terms * (scale * scale * scale) / rows.shape[1])
    )


def run_last(part, parts, before, hidden, cotangent, own, other, out_own, out_other, norm):
    tokens, width = hidden.shape
    cycle = parts * own.shape[0] // tokens
    rows = LENGTH // 4
    steps = tokens // rows // parts
    far = pl.BlockSpec((rows, width), lambda s: (s + part * steps, 0))
    near = pl.BlockSpec((rows, width), lambda s: (s + part % cycle * steps, 0))
    return pl.pallas_call(
        last_kernel,
        grid=(steps,),
        in_specs=[far, far, near, near, far, far, const_spec((8, width))]
        + [pl.BlockSpec(memory_space=pl.ANY)] * len(before),
        out_specs=[far, far],
        out_shape=[shape_of(tokens, width), shape_of(tokens, width)],
        input_output_aliases={7 + k: k for k in range(len(before))},
        compiler_params=pltpu.CompilerParams(vmem_limit_bytes=56 * MIB),
        cost_estimate=cost(5.5),
        name="grad_hidden",
    )(hidden, cotangent, own, other, out_own, out_other, norm, *before)


def join_weights_kernel(bits, own_ref, came_ref, out_ref, gate_ref):
    half = own_ref.shape[0] // 2
    join_last(bits, own_ref, came_ref, out_ref, 0, half, 0)
    join_last(bits, own_ref, came_ref, gate_ref, 0, half, half)


def join_small_kernel(bits, own_ref, came_ref, out_ref, shared_ref):
    join_last(bits, own_ref, came_ref, out_ref, 0, own_ref.shape[0])
    shared_ref[...] = out_ref[:SHARED_ROWS, :]


def finish_kernel(digits, own_ref, came_ref, small_ref, other_ref, vectors_ref, value_ref, state_ref, norm_ref,
                  step_ref, kernel_ref, offset_ref, state_kernel_ref, state_offset_ref, bias_ref, decay_ref,
                  skip_ref, gain_ref):
    heads = step_ref.shape[0]
    first = digits[digits.shape[0] - 1] == 0
    width = value_ref.shape[0]
    plan = pack_plan(width)
    half = own_ref.shape[0]
    mine = pl.ds(pl.multiple_of(digits[0] * half, 8), half)
    other = pl.ds(pl.multiple_of((1 - digits[0]) * half, 8), half)
    value_ref[mine, : 2 * WIDTH] = own_ref[...]
    value_ref[other, : 2 * WIDTH] = came_ref[...]
    for start, stop, lane in plan["value"]:
        value_ref[:, 2 * WIDTH + lane : 2 * WIDTH + lane + 128] = small_ref[start:stop, :]
    ((start, stop, _),) = plan["state"]
    here, there = small_ref[start:stop, :], other_ref[start:stop, :]
    state_ref[:, :STATE] = jnp.where(first, here, there)
    state_ref[:, STATE:] = jnp.where(first, there, here)
    ((start, stop, _),) = plan["state_rows"]
    here, there = small_ref[start:stop, :], other_ref[start:stop, :]
    rows = jnp.concatenate([jnp.where(first, here, there), jnp.where(first, there, here)], axis=1)
    state_kernel_ref[...] = rows[:TAPS]
    state_offset_ref[...] = rows[TAPS : TAPS + 1].reshape(2 * STATE)
    whole = lambda name: jnp.concatenate([small_ref[start:stop, :] for start, stop, _ in plan[name]], axis=1)
    norm = whole("norm") + jnp.concatenate([other_ref[start:stop, :] for start, stop, _ in plan["norm"]], axis=1)
    norm_ref[...] = (norm[0:1] / vectors_ref[NORM : NORM + 1, :]).reshape(width)
    step_ref[...] = whole("step")[:heads]
    rows = whole("value_rows")
    kernel_ref[...] = rows[:TAPS]
    offset_ref[...] = rows[TAPS : TAPS + 1].reshape(width)
    gain_ref[...] = whole("gain")[0:1].reshape(width)
    rows_of_heads = whole("heads")
    bias_ref[...] = rows_of_heads[0:1, :heads].reshape(heads)
    decay_ref[...] = rows_of_heads[1:2, :heads].reshape(heads)
    down = lax.broadcasted_iota(jnp.int32, (width, 128), 0)
    begin = lax.broadcasted_iota(jnp.int32, (width, 128), 1) * HEAD_DIM
    picks = jnp.where((down >= begin) & (down < begin + HEAD_DIM), 1.0, 0.0).astype(BF16)
    high, middle, low = split3(rows)
    skip_rows = dot_nn(high, picks) + dot_nn(middle, picks) + dot_nn(low, picks)
    skip_ref[...] = skip_rows[TAPS + 1 : TAPS + 2, :heads].reshape(heads)


def prepare_kernel(
    norm_ref, offset_ref, gain_ref, skip_ref, kernel_ref, state_kernel_ref, state_offset_ref, bias_ref, decay_ref,
    step_ref, vectors_ref, state_vectors_ref, heads_ref, step_rows_ref,
):
    heads = step_ref.shape[0]
    width = norm_ref.shape[0]
    row = lambda ref: ref[...].reshape(1, ref.shape[0])
    vectors_ref[NORM : NORM + 1, :] = row(norm_ref)
    vectors_ref[OFFSET : OFFSET + 1, :] = row(offset_ref)
    vectors_ref[GAIN : GAIN + 1, :] = row(gain_ref)
    vectors_ref[KERNEL : KERNEL + TAPS, :] = kernel_ref[...]
    state_vectors_ref[...] = jnp.zeros_like(state_vectors_ref)
    state_vectors_ref[:TAPS, :] = state_kernel_ref[...]
    state_vectors_ref[TAPS : TAPS + 1, :] = row(state_offset_ref)
    heads_ref[...] = jnp.zeros_like(heads_ref)
    heads_ref[0:1, :heads] = row(bias_ref)
    heads_ref[1:2, :heads] = -jnp.exp(row(decay_ref))
    heads_ref[2:3, :heads] = row(skip_ref)
    lanes = lax.broadcasted_iota(jnp.int32, (128, width), 1)
    start = lax.broadcasted_iota(jnp.int32, (128, width), 0) * HEAD_DIM
    picks = jnp.where((lanes >= start) & (lanes < start + HEAD_DIM), 1.0, 0.0).astype(BF16)
    high, middle, low = split3(heads_ref[...])
    spread_rows = dot_nn(high, picks) + dot_nn(middle, picks) + dot_nn(low, picks)
    vectors_ref[SKIP : SKIP + 1, :] = spread_rows[2:3]
    step_rows_ref[...] = jnp.concatenate(
        [step_ref[...].astype(F32), jnp.zeros((128 - heads, width), F32)], axis=0
    ).astype(BF16)


def run_prepare(*arrays):
    width = arrays[0].shape[0]
    shapes = [shape_of(8, width), shape_of(8, 2 * STATE), shape_of(8, 128), shape_of(128, width, dtype=BF16)]
    return pl.pallas_call(
        prepare_kernel,
        out_shape=shapes,
        cost_estimate=cost(2),
        name="prepare",
    )(*arrays)


SWAP = [(0, 1), (1, 0)]
IN_PARTS = 2
LAST_PARTS = 4


def swap(value):
    return lax.ppermute(value, "tensor", SWAP)


def body(hidden, cotangent, norm_weight, gate_in, value_in, state_in, step_in, value_kernel, value_offset,
         state_kernel, state_offset, step_bias, log_decay, skip_weight, gated_norm, out_weight):
    core = lax.axis_index("tensor").astype(jnp.int32)
    tokens, width = hidden.shape
    channels = gate_in.shape[1]
    heads = step_in.shape[1]
    inner = 2 * channels
    count = lax.axis_size("dp")
    core_index = core.reshape(1)
    if count & (count - 1) == 0 and width % (8 * count) == 0 and PACK_ROWS % (8 * count) == 0:
        reduction = Reduction
        position = lax.axis_index("dp").astype(jnp.int32)
        bits = [
            jnp.where(core == 0, (position >> low) & 1, (position >> high) & 1)
            for low, high in zip(*bit_orders(count), strict=True)
        ]
    else:
        reduction = PlainReduction
        bits = [jnp.int32(0)]
    digits = jnp.stack(bits + [core])
    vectors, state_vectors, head_rows, step_rows = run_prepare(
        norm_weight, value_offset, gated_norm, skip_weight, value_kernel, state_kernel, state_offset, step_bias,
        log_decay, step_in.T,
    )

    (normed, state_raw, conv, pair_t, value_raw, gate_raw, mixed, gated, grad_scaled, step_pre, steps, log, sums) = run_forward(
        hidden, cotangent, vectors, state_vectors, head_rows, gate_in, value_in, state_in, step_rows, out_weight
    )
    grad_mixed, gate_low, partial_out, grad_gain, norm_gate, *pieces = run_norm_back(
        digits, normed, gated, mixed, gate_raw, grad_scaled, cotangent, sums, swap(sums), vectors, gate_in, out_weight, inner
    )
    weights_sum = reduction(pieces, digits, count, "weights")
    other_out = swap(partial_out)
    groups = channels // WIDTH
    value_low = grad_pair = first_value = None
    row_sums, column_sums, direct, value_rows, norm_rows = [], [], [], [], [norm_gate]
    ready = normed
    for group in range(groups):
        last = group == groups - 1
        extra = (conv, step_pre, head_rows, step_rows, row_sums, column_sums, direct) if last else None
        results = list(run_scan_back(
            group, groups, digits, ready, pair_t, value_raw, grad_mixed, steps, log, vectors, value_in, value_low,
            grad_pair, first_value, extra,
        ))
        value_low = results.pop(0)
        if not last:
            grad_pair = results.pop(0)
            for kept in (row_sums, column_sums, direct):
                kept.append(results.pop(0))
        if group == 1:
            pieces = [results.pop(0), results.pop(0)]
            value_sum = reduction(pieces, digits, count, "value")
        else:
            first_value = results.pop(0)
        value_rows.append(results.pop(0))
        norm_rows.append(results.pop(0))
        ready = tie(normed, weights_sum.advance(value_low))
    step_low, mine, outgoing, grad_step, grad_heads = results
    came = swap(tie(outgoing, weights_sum.held, value_sum.advance(value_low)))
    state_low, *pieces = run_state(
        digits, core, mine, came, state_raw, ready, state_in, state_vectors, first_value, grad_step, grad_gain,
        grad_heads, value_rows, norm_rows,
    )
    small_sum = reduction(pieces, digits, count, "small")
    value_sum.advance(state_low)
    weights_sum.advance(state_low)
    partials = []
    for part in range(IN_PARTS):
        low = tie(state_low, value_sum.held, weights_sum.held, small_sum.held)
        partial_in = run_in(
            part, IN_PARTS, core_index, gate_low, value_low, step_low, low, gate_in, value_in, step_rows, state_in
        )
        partials.append((partial_in, swap(partial_in)))
        small_sum.advance(partial_in)
        value_sum.advance(partial_in)
        if part:
            weights_sum.advance(partial_in)
    results = []
    for part in range(LAST_PARTS):
        ready = tie(vectors, value_sum.held, weights_sum.held, small_sum.held)
        results = run_last(
            part, LAST_PARTS, results, hidden, cotangent, *partials[part * IN_PARTS // LAST_PARTS], partial_out,
            other_out, ready,
        )
        small_sum.advance(results[0])
        if part % 2:
            weights_sum.advance(results[0])
        else:
            value_sum.advance(results[0])
    block_out, grad_hidden = results
    grad_out_weight, grad_gate_in = small_call(
        join_weights_kernel, digits, list(weights_sum.halves()), [shape_of(channels, width), shape_of(width, channels)], "weights_last"
    )
    value_halves = value_sum.halves()
    small, shared = small_call(
        join_small_kernel, digits, list(small_sum.halves()), [shape_of(PACK_ROWS, 128), shape_of(SHARED_ROWS, 128)], "small_last"
    )
    (grad_value_in, grad_state_in, grad_norm, grad_step_in, grad_value_kernel, grad_value_offset, grad_state_kernel,
     grad_state_offset, grad_step_bias, grad_log_decay, grad_skip, grad_gain) = small_call(
        finish_kernel, digits, [*value_halves, small, swap(shared), tie(vectors, grad_out_weight)],
        [shape_of(width, channels), shape_of(width, 2 * STATE), shape_of(width), shape_of(heads, width),
         shape_of(TAPS, channels), shape_of(channels), shape_of(TAPS, 2 * STATE), shape_of(2 * STATE),
         shape_of(heads), shape_of(heads), shape_of(heads), shape_of(channels)], "finish",
    )
    return (
        block_out,
        grad_hidden,
        grad_norm,
        grad_gate_in,
        grad_value_in,
        grad_state_in,
        grad_step_in.T,
        grad_value_kernel,
        grad_value_offset,
        grad_state_kernel,
        grad_state_offset,
        grad_step_bias,
        grad_log_decay,
        grad_skip,
        grad_gain,
        grad_out_weight,
    )


def solution(mesh):
    in_specs = (
        P("dp", None),
        P("dp", None),
        P(),
        P(None, "tensor"),
        P(None, "tensor"),
        P(),
        P(None, "tensor"),
        P(None, "tensor"),
        P("tensor"),
        P(),
        P(),
        P("tensor"),
        P("tensor"),
        P("tensor"),
        P("tensor"),
        P("tensor", None),
    )
    out_specs = (
        P("dp", None),
        P("dp", None),
        P(),
        P(None, "tensor"),
        P(None, "tensor"),
        P(),
        P(None, "tensor"),
        P(None, "tensor"),
        P("tensor"),
        P(),
        P(),
        P("tensor"),
        P("tensor"),
        P("tensor"),
        P("tensor"),
        P("tensor", None),
    )
    return jax.shard_map(body, mesh=mesh, in_specs=in_specs, out_specs=out_specs, check_vma=False)
```

time: 444 us -> 318 us (0.72)
  waiting for transfers between devices: 165 us -> 79.9 us
  blocking collectives: 68.5 us -> 0 us
  Pallas kernels: 167 us -> 210 us
  starting transfers between devices: 1.7 us -> 24.5 us
  local copies, waits for them, and re-layouts: 20.3 us -> 2.22 us
  between operations: 14.2 us -> 1.24 us
  other arithmetic: 7.18 us -> 0 us
    psum x1 -> x0, waiting for transfers between devices: 142 us -> none  [body(): lax.psum((grad_out_weight, grad_gate_in, grad_value, grad_state_in, grad_...]
    ppermute x0 -> x24, waiting for transfers between devices: none -> 76.8 us  [send(): self.came = lax.ppermute(self.sent, ('dp', 'tensor'), pairs)]
    psum x1 -> x0, blocking collectives: 68.5 us -> none  [body(): lax.psum((grad_out_weight, grad_gate_in, grad_value, grad_state_in, grad_...]
    pallas_call x4 -> x34, Pallas kernels: 110 us -> 148 us  [the longest x3 66.4 us: run_scan_back(): pl.pallas_call(functools.partial(scan_back_kernel, group, groups), grid_s...]
    ppermute x0 -> x24, starting transfers between devices: none -> 22.8 us  [send(): self.came = lax.ppermute(self.sent, ('dp', 'tensor'), pairs)]
    ppermute x5 -> x6, waiting for transfers between devices: 22.8 us -> 3.08 us  [swap(): return lax.ppermute(value, 'tensor', SWAP)]
    unnamed x21 -> x22, local copies, waits for them, and re-layouts: 9.31 us -> 1.62 us
    pallas_call x1, Pallas kernels: 41.8 us -> 46.8 us  [run_forward(): pl.pallas_call(forward_kernel, grid=(sequences, groups), in_specs=[pl.Blo...]
  transfers between devices with their start and end apart: 6 -> 30, of which waited for: 5 -> 11; matrix products, arithmetic and copies ran while one was open for 2% -> 0% of each run, Pallas kernels for 4% -> 40%
where the time goes in v2:
time: 318 us
  Pallas kernels  210 us (66%)
  waiting for transfers between devices  79.9 us (25%)
  starting transfers between devices  24.5 us (8%)
    ppermute x24, waiting for transfers between devices, send(): self.came = lax.ppermute(self.sent, ('dp', 'tensor'), pairs)  76.8 us
    pallas_call x3, Pallas kernels, run_scan_back(): pl.pallas_call(functools.partial(scan_back_kernel, group, groups), grid_s...  66.4 us
    pallas_call x1, Pallas kernels, run_forward(): pl.pallas_call(forward_kernel, grid=(sequences, groups), in_specs=[pl.Blo...  46.8 us
    pallas_call x1, Pallas kernels, run_norm_back(): pl.pallas_call(functools.partial(norm_back_kernel, inner), grid_spec=pltp...  26 us
    pallas_call x4, Pallas kernels, run_last(): pl.pallas_call(last_kernel, grid=(steps,), in_specs=[far, far, near, near...  23.3 us
    ppermute x24, starting transfers between devices, send(): self.came = lax.ppermute(self.sent, ('dp', 'tensor'), pairs)  22.8 us
    pallas_call x24, Pallas kernels, small_call(): pl.pallas_call(kernel, grid_spec=pltpu.PrefetchScalarGridSpec(num_scalar_...  22.4 us
    pallas_call x2, Pallas kernels, run_in(): pl.pallas_call(in_kernel, grid_spec=pltpu.PrefetchScalarGridSpec(num_scal...  14.9 us
  transfers between devices with their start and end apart: 30, of which 11 were waited for; matrix products, arithmetic and copies ran while one was open for 0% of the time, Pallas kernels for 40%

profile of v2, /device:TPU:1, one launch (start us, length us, event | category | flops | bytes accessed | tf_op | source)
XLA Modules:
  0.0 317.7 jit_solution(6311813143718075099)
XLA Ops:
  0.6 1.7 prepare.1
  2.4 46.8 %forward_mix.1 = (bf16[2048,768]{1,0:T(8,128)(2,1)}, f32[2048,256]{1,0:T(8,128)}, f32[2048,256]{1,0:T(8,128)}, f32[2048,512]{1,0:T(8,128)}, f32[2048,768]{1,0:T(...) custom-call(f32[2048,768]{1,0:T(8,128)} %hidden_ref.9, ...), custom_call_target="tpu_custom_call" | custom-call | flops 134999998464 | bytes 405000000 | tf_op jit(solution)/shard_map/forward_mix/pallas_call | solution.py:369
  51.3 26.0 %norm_back.1 = (f32[2048,768]{1,0:T(8,128)}, bf16[2048,768]{1,0:T(8,128)(2,1)}, f32[2048,768]{1,0:T(8,128)}, f32[8,768]{1,0:T(8,128)}, f32[8,768]{1,0:T(8,128)}, /*index=5*/f32[768,768]{1,0:T(8,128)}, f32[768,768]{1,0:T(8,128)}) custom-call(s32[5]{0:T(128)} %stack.20.digits.bits, bf16[2048,768]{1,0:T(8,128)(2,1)} %get-tuple-element.192.normed_ref, ...), custom_call_target="tpu_custom_call" | custom-call | flops 77999996928 | bytes 234000000 | tf_op jit(solution)/shard_map/norm_back/pallas_call | solution.py:497
  77.4 2.5 collective-permute-start.1
  79.8 20.4 %scan_back.3 = (bf16[2048,768]{1,0:T(8,128)(2,1)}, f32[2048,512]{1,0:T(8,128)}, f32[8,2048]{1,0:T(8,128)}, f32[2048,128]{1,0:T(8,128)}, f32[2048,128]{1,0:T(8,12...) custom-call(s32[5]{0:T(128)} %stack.20.digits.bits, bf16[2048,768]{1,0:T(8,128)(2,1)} %get-tuple-element.192.normed_ref, ...), custom_call_target="tpu_custom_call" | custom-call | flops 65999998976 | bytes 198000000 | tf_op jit(solution)/shard_map/scan_back/pallas_call | solution.py:753
  100.2 6.4 %collective-permute-done.1.came_ref = f32[768,768]{1,0:T(8,128)} collective-permute-done((f32[768,768]{1,0:T(8,128)}, f32[768,768]{1,0:T(8,128)}, u32[]{:S(2)}, u32[]{:S(2)}) %collective-permute-start.1) | collective-permute-done | bytes 2359328 | tf_op jit(solution)/shard_map/ppermute | solution.py:309
  106.7 3.5 %weights_sum.3 = (f32[384,768]{1,0:T(8,128)}, f32[384,768]{1,0:T(8,128)S(1)}) custom-call(s32[5]{0:T(128)S(1)} %copy-done.3, f32[768,768]{1,0:T(8,128)S(1)} %copy-done, f32[768,768]{1,0:T(8,128)} %collective-permute-done.1.came_ref), custom_call_target="tpu_custom_call" | custom-call | flops 300000000 | bytes 900000 | tf_op jit(solution)/shard_map/weights_sum/pallas_call | solution.py:276
  110.1 1.5 collective-permute-start.2
  111.6 21.8 %scan_back.4 = (bf16[2048,768]{1,0:T(8,128)(2,1)}, f32[2048,512]{1,0:T(8,128)}, f32[8,2048]{1,0:T(8,128)}, f32[2048,128]{1,0:T(8,128)}, f32[2048,128]{1,0:T(8,12...) custom-call(s32[5]{0:T(128)} %stack.20.digits.bits, ...), custom_call_target="tpu_custom_call", output_to_operand_aliasing={{0}: (9, {})} | custom-call | flops 65999998976 | bytes 198000000 | tf_op jit(solution)/shard_map/scan_back/pallas_call | solution.py:753
  134.7 1.5 weights_sum.4
  136.3 2.3 collective-permute-start.3
  138.6 24.3 %scan_back.5 = (bf16[2048,768]{1,0:T(8,128)(2,1)}, f32[768,256]{1,0:T(8,128)}, f32[8,256]{1,0:T(8,128)}, f32[8,768]{1,0:T(8,128)}, bf16[2048,128]{1,0:T(8,128)(2...) custom-call(s32[5]{0:T(128)} %stack.20.digits.bits, ...), custom_call_target="tpu_custom_call", output_to_operand_aliasing={{0}: (9, {})} | custom-call | flops 65999998976 | bytes 198000000 | tf_op jit(solution)/shard_map/scan_back/pallas_call | solution.py:753
  166.1 2.3 collective-permute-done.5.came_ref
  169.4 8.2 %state_back.1 = (bf16[2048,128]{1,0:T(8,128)(2,1)}, f32[1280,128]{1,0:T(8,128)}, f32[1280,128]{1,0:T(8,128)}) custom-call(s32[5]{0:T(128)} %stack.20.digits.bits, f32[2048,128]{1,0:T(8,128)} %get-tuple-element.181.mine_ref, f32[2048,128]{1,0:T(8,128)} %copy-done.8, f32[2048,256]{1,0:T(8,128)} %get-tuple-element.191.raw_ref, ...), custom_call_target="tpu_custom_call" | custom-call | flops 24000000000 | bytes 72000000 | tf_op jit(solution)/shard_map/state_back/pallas_call | solution.py:836
  178.8 7.5 %grad_in.2.own_ref = f32[1024,768]{1,0:T(8,128)} custom-call(s32[1]{0:T(128)} %bitcast.core, bf16[2048,768]{1,0:T(8,128)(2,1)} %get-tuple-element.151.gate_low_ref, bf16[2048,768]{1,0:T(8,128)(2,1)} %get-tuple-element.179.value_low_ref, bf16[2048,128]{1,0:T(8,128)(2,1)} %get-tuple-element.180.step_low_ref, ...), custom_call_target="tpu_custom_call" | custom-call | flops 22499999744 | bytes 67500000 | tf_op jit(solution)/shard_map/grad_in/pallas_call | solution.py:879
  189.5 12.4 %collective-permute-done.8.came_ref = f32[96,512]{1,0:T(8,128)S(1)} collective-permute-done((f32[96,512]{1,0:T(8,128)S(1)}, f32[96,512]{1,0:T(8,128)S(1)}, u32[]{:S(2)}, u32[]{:S(2)}) %collective-permute-start.8) | collective-permute-done | bytes 196640 | tf_op jit(solution)/shard_map/ppermute | solution.py:309
  203.5 7.4 %grad_in.3.own_ref = f32[1024,768]{1,0:T(8,128)} custom-call(s32[1]{0:T(128)} %bitcast.core, bf16[2048,768]{1,0:T(8,128)(2,1)} %get-tuple-element.151.gate_low_ref, bf16[2048,768]{1,0:T(8,128)(2,1)} %get-tuple-element.179.value_low_ref, bf16[2048,128]{1,0:T(8,128)(2,1)} %get-tuple-element.180.step_low_ref, ...), custom_call_target="tpu_custom_call" | custom-call | flops 22499999744 | bytes 67500000 | tf_op jit(solution)/shard_map/grad_in/pallas_call | solution.py:879
  214.1 2.4 collective-permute-start.17
  216.5 5.8 %grad_hidden.4 = (f32[2048,768]{1,0:T(8,128)}, f32[2048,768]{1,0:T(8,128)}) custom-call(f32[2048,768]{1,0:T(8,128)} %hidden_ref.9, f32[2048,768]{1,0:T(8,128)} %cotangent_ref.11, f32[1024,768]{1,0:T(8,128)} %grad_in.2.own_ref, f32[1024,768]{1,0:T(8,128)} %collective-permute-done.13.other_ref, f32[2048,768]{1,0:T(8,128)} %get-tuple-element.219.out_own_ref, ...), custom_call_target="tpu_custom_call" | custom-call | flops 16499999744 | bytes 49500000 | tf_op jit(solution)/shard_map/grad_hidden/pallas_call | solution.py:922
  222.3 11.8 %collective-permute-done.17.came_ref = f32[320,128]{1,0:T(8,128)S(1)} collective-permute-done((f32[320,128]{1,0:T(8,128)S(1)}, f32[320,128]{1,0:T(8,128)S(1)}, u32[]{:S(2)}, u32[]{:S(2)}) %collective-permute-start.17) | collective-permute-done | bytes 163872 | tf_op jit(solution)/shard_map/ppermute | solution.py:309
  236.6 5.9 %grad_hidden.5 = (f32[2048,768]{1,0:T(8,128)}, f32[2048,768]{1,0:T(8,128)}) custom-call(f32[2048,768]{1,0:T(8,128)} %hidden_ref.9, f32[2048,768]{1,0:T(8,128)} %cotangent_ref.11, f32[1024,768]{1,0:T(8,128)} %grad_in.2.own_ref, f32[1024,768]{1,0:T(8,128)} %collective-permute-done.13.other_ref, ...), custom_call_target="tpu_custom_call", output_to_operand_aliasing={{0}: (7, {}), {1}: (8, {})} | custom-call | flops 16499999744 | bytes 49500000 | tf_op jit(solution)/shard_map/grad_hidden/pallas_call | solution.py:922
  245.3 5.9 %grad_hidden.6 = (f32[2048,768]{1,0:T(8,128)}, f32[2048,768]{1,0:T(8,128)}) custom-call(f32[2048,768]{1,0:T(8,128)} %hidden_ref.9, f32[2048,768]{1,0:T(8,128)} %cotangent_ref.11, f32[1024,768]{1,0:T(8,128)} %grad_in.3.own_ref, f32[1024,768]{1,0:T(8,128)} %collective-permute-done.10.other_ref, ...), custom_call_target="tpu_custom_call", output_to_operand_aliasing={{0}: (7, {}), {1}: (8, {})} | custom-call | flops 16499999744 | bytes 49500000 | tf_op jit(solution)/shard_map/grad_hidden/pallas_call | solution.py:922
  252.3 5.8 %grad_hidden.7 = (f32[2048,768]{1,0:T(8,128)}, f32[2048,768]{1,0:T(8,128)}) custom-call(f32[2048,768]{1,0:T(8,128)} %hidden_ref.9, f32[2048,768]{1,0:T(8,128)} %cotangent_ref.11, f32[1024,768]{1,0:T(8,128)} %grad_in.3.own_ref, f32[1024,768]{1,0:T(8,128)} %collective-permute-done.10.other_ref, ...), custom_call_target="tpu_custom_call", output_to_operand_aliasing={{0}: (7, {}), {1}: (8, {})} | custom-call | flops 16499999744 | bytes 49500000 | tf_op jit(solution)/shard_map/grad_hidden/pallas_call | solution.py:922
  258.1 5.2 %collective-permute-done.28.came_ref = f32[384,768]{1,0:T(8,128)S(1)} collective-permute-done((f32[384,768]{1,0:T(8,128)S(1)}, f32[384,768]{1,0:T(8,128)S(1)}, u32[]{:S(2)}, u32[]{:S(2)}) %collective-permute-start.28) | collective-permute-done | bytes 1179680 | tf_op jit(solution)/shard_map/ppermute | solution.py:309
  264.2 6.4 %collective-permute-done.24.came_ref = f32[320,128]{1,0:T(8,128)S(1)} collective-permute-done((f32[320,128]{1,0:T(8,128)S(1)}, f32[320,128]{1,0:T(8,128)S(1)}, u32[]{:S(2)}, u32[]{:S(2)}) %collective-permute-start.24) | collective-permute-done | bytes 163872 | tf_op jit(solution)/shard_map/ppermute | solution.py:309
  271.2 1.5 collective-permute-start.22
  272.7 4.8 %collective-permute-done.25.came_ref = f32[640,128]{1,0:T(8,128)S(1)} collective-permute-done((f32[640,128]{1,0:T(8,128)S(1)}, f32[640,128]{1,0:T(8,128)S(1)}, u32[]{:S(2)}, u32[]{:S(2)}) %collective-permute-start.25) | collective-permute-done | bytes 327712 | tf_op jit(solution)/shard_map/ppermute | solution.py:309
  279.4 2.2 collective-permute-done.22.came_ref
  283.6 22.9 %collective-permute-done.26.came_ref = f32[1280,128]{1,0:T(8,128)S(1)} collective-permute-done((f32[1280,128]{1,0:T(8,128)S(1)}, f32[1280,128]{1,0:T(8,128)S(1)}, u32[]{:S(2)}, u32[]{:S(2)}) %collective-permute-start.26) | collective-permute-done | bytes 655392 | tf_op jit(solution)/shard_map/ppermute | solution.py:309
  307.3 3.0 weights_last.1
  310.3 4.6 %collective-permute-done.23.came_ref = f32[384,512]{1,0:T(8,128)S(1)} collective-permute-done((f32[384,512]{1,0:T(8,128)S(1)}, f32[384,512]{1,0:T(8,128)S(1)}, u32[]{:S(2)}, u32[]{:S(2)}) %collective-permute-start.23) | collective-permute-done | bytes 786464 | tf_op jit(solution)/shard_map/ppermute | solution.py:309
  315.0 2.5 finish.1
  (88 shorter events, 29.3 us)
Async XLA Ops:
  49.2 1.5 collective-permute-start
  77.4 29.3 %collective-permute-start.1 = (f32[768,768]{1,0:T(8,128)}, f32[768,768]{1,0:T(8,128)}, u32[]{:S(2)}, u32[]{:S(2)}) collective-permute-start(f32[768,768]{1,0:T(8,128)} %get-tuple-element.160), channel_id=1, source_target_pairs={{0,2},{1,5},{2,0},{3,7},{4,6},{5,1},{6,4},{7,3},{8,10},{9,13},{10,... | collective-permute-start | bytes 7077896 | tf_op jit(solution)/shard_map/ppermute | solution.py:309
  79.8 26.8 %copy-start.3 = (s32[5]{0:T(128)S(1)}, s32[5]{0:T(128)}, u32[]{:S(2)}) copy-start(s32[5]{0:T(128)} %stack.20.digits.bits) | copy-start | bytes 64
  110.1 24.6 %collective-permute-start.2 = (f32[384,768]{1,0:T(8,128)}, f32[384,768]{1,0:T(8,128)S(1)}, u32[]{:S(2)}, u32[]{:S(2)}) collective-permute-start(f32[384,768]{1,0:T(8,128)} %get-tuple-element.167), channel_id=1, source_target_pairs={{0,4},{1,9},{2,6},{3,11},{4,0},{5,13},{6,2},{7,15},{8,12},{9,1},{1... | collective-permute-start | bytes 3538952 | tf_op jit(solution)/shard_map/ppermute | solution.py:309
  133.4 29.4 %collective-permute-start.4 = (f32[384,512]{1,0:T(8,128)}, f32[384,512]{1,0:T(8,128)S(1)}, u32[]{:S(2)}, u32[]{:S(2)}) collective-permute-start(f32[384,512]{1,0:T(8,128)} %get-tuple-element.188), channel_id=1, source_target_pairs={{0,2},{1,5},{2,0},{3,7},{4,6},{5,1},{6,4},{7,3},{8,10},{9,13},{10,... | collective-permute-start | bytes 2359304 | tf_op jit(solution)/shard_map/ppermute | solution.py:309
  136.3 27.2 %collective-permute-start.3 = (f32[192,768]{1,0:T(8,128)}, f32[192,768]{1,0:T(8,128)S(1)}, u32[]{:S(2)}, u32[]{:S(2)}) collective-permute-start(f32[192,768]{1,0:T(8,128)} %get-tuple-element.184), channel_id=1, source_target_pairs={{0,8},{1,17},{2,10},{3,19},{4,12},{5,21},{6,14},{7,23},{8,0},{9,25... | collective-permute-start | bytes 1769480 | tf_op jit(solution)/shard_map/ppermute | solution.py:309
  164.2 4.2 %collective-permute-start.5 = (f32[2048,128]{1,0:T(8,128)}, f32[2048,128]{1,0:T(8,128)S(1)}, u32[]{:S(2)}, u32[]{:S(2)}) collective-permute-start(f32[2048,128]{1,0:T(8,128)} %get-tuple-element.190), channel_id=1, source_target_pairs={{0,1},{1,0},{2,3},{3,2},{4,5},{5,4},{6,7},{7,6},{8,9},{9,8},{10,11... | collective-permute-start | bytes 3145736 | tf_op jit(solution)/shard_map/ppermute | solution.py:1035
  165.2 48.9 %collective-permute-start.11 = (f32[2048,768]{1,0:T(8,128)}, f32[2048,768]{1,0:T(8,128)}, u32[]{:S(2)}, u32[]{:S(2)}) collective-permute-start(f32[2048,768]{1,0:T(8,128)} %get-tuple-element.219.out_own_ref), channel_id=1, source_target_pairs={{0,1},{1,0},{2,3},{3,2},{4,5},{5,4},{6,7},{7,6},{8,9},{9,8},{10,11... | collective-permute-start | bytes 18874376 | tf_op jit(solution)/shard_map/ppermute | solution.py:1035
  165.3 12.9 %collective-permute-start.6 = (f32[192,512]{1,0:T(8,128)S(1)}, f32[192,512]{1,0:T(8,128)S(1)}, u32[]{:S(2)}, u32[]{:S(2)}) collective-permute-start(f32[192,512]{1,0:T(8,128)S(1)} %get-tuple-element.206), channel_id=1, source_target_pairs={{0,4},{1,9},{2,6},{3,11},{4,0},{5,13},{6,2},{7,15},{8,12},{9,1},{1... | collective-permute-start | bytes 1179656 | tf_op jit(solution)/shard_map/ppermute | solution.py:309
  165.4 12.1 %collective-permute-start.7 = (f32[96,768]{1,0:T(8,128)S(1)}, f32[96,768]{1,0:T(8,128)S(1)}, u32[]{:S(2)}, u32[]{:S(2)}) collective-permute-start(f32[96,768]{1,0:T(8,128)S(1)} %get-tuple-element.209), channel_id=1, source_target_pairs={{0,16},{1,3},{2,18},{3,1},{4,20},{5,7},{6,22},{7,5},{8,24},{9,11},... | collective-permute-start | bytes 884744 | tf_op jit(solution)/shard_map/ppermute | solution.py:309
  186.3 30.3 %collective-permute-start.13 = (f32[1024,768]{1,0:T(8,128)}, f32[1024,768]{1,0:T(8,128)}, u32[]{:S(2)}, u32[]{:S(2)}) collective-permute-start(f32[1024,768]{1,0:T(8,128)} %grad_in.2.own_ref), channel_id=1, source_target_pairs={{0,1},{1,0},{2,3},{3,2},{4,5},{5,4},{6,7},{7,6},{8,9},{9,8},{10,11... | collective-permute-start | bytes 9437192 | tf_op jit(solution)/shard_map/ppermute | solution.py:1035
  186.7 16.1 %collective-permute-start.9 = (f32[1280,128]{1,0:T(8,128)S(1)}, f32[1280,128]{1,0:T(8,128)S(1)}, u32[]{:S(2)}, u32[]{:S(2)}) collective-permute-start(f32[1280,128]{1,0:T(8,128)S(1)} %copy-done.9), channel_id=1, source_target_pairs={{0,2},{1,5},{2,0},{3,7},{4,6},{5,1},{6,4},{7,3},{8,10},{9,13},{10,... | collective-permute-start | bytes 1966088 | tf_op jit(solution)/shard_map/ppermute | solution.py:309
  187.9 14.0 %collective-permute-start.8 = (f32[96,512]{1,0:T(8,128)S(1)}, f32[96,512]{1,0:T(8,128)S(1)}, u32[]{:S(2)}, u32[]{:S(2)}) collective-permute-start(f32[96,512]{1,0:T(8,128)S(1)} %get-tuple-element.213), channel_id=1, source_target_pairs={{0,8},{1,17},{2,10},{3,19},{4,12},{5,21},{6,14},{7,23},{8,0},{9,25... | collective-permute-start | bytes 589832 | tf_op jit(solution)/shard_map/ppermute | solution.py:309
  189.2 22.3 %collective-permute-start.14 = (f32[96,768]{1,0:T(8,128)S(1)}, f32[96,768]{1,0:T(8,128)S(1)}, u32[]{:S(2)}, u32[]{:S(2)}) collective-permute-start(f32[96,768]{1,0:T(8,128)S(1)} %weights_total.1.own_ref), channel_id=1, source_target_pairs={{0,16},{1,3},{2,18},{3,1},{4,20},{5,7},{6,22},{7,5},{8,24},{9,11},... | collective-permute-start | bytes 884744 | tf_op jit(solution)/shard_map/ppermute | solution.py:309
  202.5 8.4 %collective-permute-start.12 = (f32[48,512]{1,0:T(8,128)S(1)}, f32[48,512]{1,0:T(8,128)S(1)}, u32[]{:S(2)}, u32[]{:S(2)}) collective-permute-start(f32[48,512]{1,0:T(8,128)S(1)} %get-tuple-element.221), channel_id=1, source_target_pairs={{0,16},{1,3},{2,18},{3,1},{4,20},{5,7},{6,22},{7,5},{8,24},{9,11},... | collective-permute-start | bytes 294920 | tf_op jit(solution)/shard_map/ppermute | solution.py:309
  203.4 10.0 %collective-permute-start.15 = (f32[640,128]{1,0:T(8,128)S(1)}, f32[640,128]{1,0:T(8,128)S(1)}, u32[]{:S(2)}, u32[]{:S(2)}) collective-permute-start(f32[640,128]{1,0:T(8,128)S(1)} %get-tuple-element.224), channel_id=1, source_target_pairs={{0,4},{1,9},{2,6},{3,11},{4,0},{5,13},{6,2},{7,15},{8,12},{9,1},{1... | collective-permute-start | bytes 983048 | tf_op jit(solution)/shard_map/ppermute | solution.py:309
  210.9 34.4 %collective-permute-start.10 = (f32[1024,768]{1,0:T(8,128)}, f32[1024,768]{1,0:T(8,128)}, u32[]{:S(2)}, u32[]{:S(2)}) collective-permute-start(f32[1024,768]{1,0:T(8,128)} %grad_in.3.own_ref), channel_id=1, source_target_pairs={{0,1},{1,0},{2,3},{3,2},{4,5},{5,4},{6,7},{7,6},{8,9},{9,8},{10,11... | collective-permute-start | bytes 9437192 | tf_op jit(solution)/shard_map/ppermute | solution.py:1035
  211.5 23.1 %collective-permute-start.16 = (f32[48,512]{1,0:T(8,128)S(1)}, f32[48,512]{1,0:T(8,128)S(1)}, u32[]{:S(2)}, u32[]{:S(2)}) collective-permute-start(f32[48,512]{1,0:T(8,128)S(1)} %value_total.1.own_ref), channel_id=1, source_target_pairs={{0,16},{1,3},{2,18},{3,1},{4,20},{5,7},{6,22},{7,5},{8,24},{9,11},... | collective-permute-start | bytes 294920 | tf_op jit(solution)/shard_map/ppermute | solution.py:309
  213.4 29.0 %collective-permute-start.18 = (f32[192,768]{1,0:T(8,128)S(1)}, f32[192,768]{1,0:T(8,128)S(1)}, u32[]{:S(2)}, u32[]{:S(2)}) collective-permute-start(f32[192,768]{1,0:T(8,128)S(1)} %weights_join.3.own_ref), channel_id=1, source_target_pairs={{0,8},{1,17},{2,10},{3,19},{4,12},{5,21},{6,14},{7,23},{8,0},{9,25... | collective-permute-start | bytes 1769480 | tf_op jit(solution)/shard_map/ppermute | solution.py:309
  214.1 20.0 %collective-permute-start.17 = (f32[320,128]{1,0:T(8,128)S(1)}, f32[320,128]{1,0:T(8,128)S(1)}, u32[]{:S(2)}, u32[]{:S(2)}) collective-permute-start(f32[320,128]{1,0:T(8,128)S(1)} %get-tuple-element.230), channel_id=1, source_target_pairs={{0,8},{1,17},{2,10},{3,19},{4,12},{5,21},{6,14},{7,23},{8,0},{9,25... | collective-permute-start | bytes 491528 | tf_op jit(solution)/shard_map/ppermute | solution.py:309
  235.3 8.9 %collective-permute-start.19 = (f32[160,128]{1,0:T(8,128)S(1)}, f32[160,128]{1,0:T(8,128)S(1)}, u32[]{:S(2)}, u32[]{:S(2)}) collective-permute-start(f32[160,128]{1,0:T(8,128)S(1)} %get-tuple-element.237), channel_id=1, source_target_pairs={{0,16},{1,3},{2,18},{3,1},{4,20},{5,7},{6,22},{7,5},{8,24},{9,11},... | collective-permute-start | bytes 245768 | tf_op jit(solution)/shard_map/ppermute | solution.py:309
  242.5 9.3 %collective-permute-start.20 = (f32[96,512]{1,0:T(8,128)S(1)}, f32[96,512]{1,0:T(8,128)S(1)}, u32[]{:S(2)}, u32[]{:S(2)}) collective-permute-start(f32[96,512]{1,0:T(8,128)S(1)} %value_join.3.own_ref), channel_id=1, source_target_pairs={{0,8},{1,17},{2,10},{3,19},{4,12},{5,21},{6,14},{7,23},{8,0},{9,25... | collective-permute-start | bytes 589832 | tf_op jit(solution)/shard_map/ppermute | solution.py:309
  243.1 20.2 %collective-permute-start.28 = (f32[384,768]{1,0:T(8,128)S(1)}, f32[384,768]{1,0:T(8,128)S(1)}, u32[]{:S(2)}, u32[]{:S(2)}) collective-permute-start(f32[384,768]{1,0:T(8,128)S(1)} %weights_join.4.own_ref), channel_id=1, source_target_pairs={{0,4},{1,9},{2,6},{3,11},{4,0},{5,13},{6,2},{7,15},{8,12},{9,1},{1... | collective-permute-start | bytes 3538952 | tf_op jit(solution)/shard_map/ppermute | solution.py:309
  244.7 6.4 %collective-permute-start.21 = (f32[160,128]{1,0:T(8,128)S(1)}, f32[160,128]{1,0:T(8,128)S(1)}, u32[]{:S(2)}, u32[]{:S(2)}) collective-permute-start(f32[160,128]{1,0:T(8,128)S(1)} %small_total.1.own_ref), channel_id=1, source_target_pairs={{0,16},{1,3},{2,18},{3,1},{4,20},{5,7},{6,22},{7,5},{8,24},{9,11},... | collective-permute-start | bytes 245768 | tf_op jit(solution)/shard_map/ppermute | solution.py:309
  264.0 43.3 %collective-permute-start.29 = (f32[768,768]{1,0:T(8,128)S(1)}, f32[768,768]{1,0:T(8,128)S(1)}, u32[]{:S(2)}, u32[]{:S(2)}) collective-permute-start(f32[768,768]{1,0:T(8,128)S(1)} %weights_join.5.own_ref), channel_id=1, source_target_pairs={{0,2},{1,5},{2,0},{3,7},{4,6},{5,1},{6,4},{7,3},{8,10},{9,13},{10,... | collective-permute-start | bytes 7077896 | tf_op jit(solution)/shard_map/ppermute | solution.py:309
  264.1 6.5 %collective-permute-start.24 = (f32[320,128]{1,0:T(8,128)S(1)}, f32[320,128]{1,0:T(8,128)S(1)}, u32[]{:S(2)}, u32[]{:S(2)}) collective-permute-start(f32[320,128]{1,0:T(8,128)S(1)} %small_join.3.own_ref), channel_id=1, source_target_pairs={{0,8},{1,17},{2,10},{3,19},{4,12},{5,21},{6,14},{7,23},{8,0},{9,25... | collective-permute-start | bytes 491528 | tf_op jit(solution)/shard_map/ppermute | solution.py:309
  271.1 6.3 %collective-permute-start.25 = (f32[640,128]{1,0:T(8,128)S(1)}, f32[640,128]{1,0:T(8,128)S(1)}, u32[]{:S(2)}, u32[]{:S(2)}) collective-permute-start(f32[640,128]{1,0:T(8,128)S(1)} %small_join.4.own_ref), channel_id=1, source_target_pairs={{0,4},{1,9},{2,6},{3,11},{4,0},{5,13},{6,2},{7,15},{8,12},{9,1},{1... | collective-permute-start | bytes 983048 | tf_op jit(solution)/shard_map/ppermute | solution.py:309
  271.2 10.4 %collective-permute-start.22 = (f32[192,512]{1,0:T(8,128)S(1)}, f32[192,512]{1,0:T(8,128)S(1)}, u32[]{:S(2)}, u32[]{:S(2)}) collective-permute-start(f32[192,512]{1,0:T(8,128)S(1)} %value_join.4.own_ref), channel_id=1, source_target_pairs={{0,4},{1,9},{2,6},{3,11},{4,0},{5,13},{6,2},{7,15},{8,12},{9,1},{1... | collective-permute-start | bytes 1179656 | tf_op jit(solution)/shard_map/ppermute | solution.py:309
  278.0 28.5 %collective-permute-start.26 = (f32[1280,128]{1,0:T(8,128)S(1)}, f32[1280,128]{1,0:T(8,128)S(1)}, u32[]{:S(2)}, u32[]{:S(2)}) collective-permute-start(f32[1280,128]{1,0:T(8,128)S(1)} %small_join.5.own_ref), channel_id=1, source_target_pairs={{0,2},{1,5},{2,0},{3,7},{4,6},{5,1},{6,4},{7,3},{8,10},{9,13},{10,... | collective-permute-start | bytes 1966088 | tf_op jit(solution)/shard_map/ppermute | solution.py:309
  282.2 32.7 %copy-start.7 = (f32[8,768]{1,0:T(8,128)S(1)}, f32[8,768]{1,0:T(8,128)}, u32[]{:S(2)}) copy-start(f32[8,768]{1,0:T(8,128)} %get-tuple-element.252.norm_ref.vectors_ref) | copy-start | bytes 73732
  282.2 32.7 %collective-permute-start.23 = (f32[384,512]{1,0:T(8,128)S(1)}, f32[384,512]{1,0:T(8,128)S(1)}, u32[]{:S(2)}, u32[]{:S(2)}) collective-permute-start(f32[384,512]{1,0:T(8,128)S(1)} %value_join.5.own_ref), channel_id=1, source_target_pairs={{0,2},{1,5},{2,0},{3,7},{4,6},{5,1},{6,4},{7,3},{8,10},{9,13},{10,... | collective-permute-start | bytes 2359304 | tf_op jit(solution)/shard_map/ppermute | solution.py:309
  307.2 7.8 %collective-permute-start.27 = (f32[824,128]{1,0:T(8,128)S(1)}, f32[824,128]{1,0:T(8,128)S(1)}, u32[]{:S(2)}, u32[]{:S(2)}) collective-permute-start(f32[824,128]{1,0:T(8,128)S(1)} %get-tuple-element.249), channel_id=1, source_target_pairs={{0,1},{1,0},{2,3},{3,2},{4,5},{5,4},{6,7},{7,6},{8,9},{9,8},{10,11... | collective-permute-start | bytes 1265672 | tf_op jit(solution)/shard_map/ppermute | solution.py:1035
  (9 other events, 140.2 us)
